TPU v7x, 128 devices: a whole 4x4x4 slice. The times are simulated.
128 devices in a mesh: tower: 16 (over z, x_lo, core), dev: 8 (over x_hi, y).
Axes of the slice: x: 4 (x_hi: 2, x_lo: 2; x = x_hi * 2 + x_lo), y: 4, z: 4, core: 2. Of those that a mesh axis runs over, the one named last changes fastest.
Arguments:
- embeddings: bfloat16 [8192, 32768], P(None, ('tower', 'dev')), may hold values from -6 to 6
- tower_v: bfloat16 [16, 2048, 256], P('tower'), may hold values from -0.125 to 0.125
- tower_u: bfloat16 [16, 256, 2048], P('tower'), may hold values from -0.375 to 0.375
- cross_bias: float32 [16, 2048], P('tower'), may hold values from -3 to 3
- proj_w: bfloat16 [16, 2048, 128], P('tower'), may hold values from -0.125 to 0.125
- proj_bias: float32 [16, 128], P('tower'), may hold values from -3 to 3
- arch_v: bfloat16 [2048, 512], replicated, may hold values from -0.125 to 0.125
- arch_u: bfloat16 [512, 2048], replicated, may hold values from -0.25 to 0.25
- arch_bias: float32 [2048], replicated, may hold values from -3 to 3
- logit_w: float32 [2048], replicated, may hold values from -0.125 to 0.125
- labels: float32 [8192], P(('tower', 'dev')), may hold values from 0 to 1
Outputs:
- emb_grad: bfloat16 [8192, 32768], P(None, ('tower', 'dev'))
- grad_tower_v: float32 [16, 2048, 256], P('tower', 'dev')
- grad_tower_u: float32 [16, 256, 2048], P('tower', 'dev')
- grad_cross_bias: float32 [16, 2048], P('tower', 'dev')
- grad_proj_w: float32 [16, 2048, 128], P('tower', 'dev')
- grad_proj_bias: float32 [16, 128], P('tower', 'dev')
- grad_arch_v: float32 [2048, 512], P(('tower', 'dev'))
- grad_arch_u: float32 [512, 2048], P(('tower', 'dev'))
- grad_arch_bias: float32 [2048], P(('tower', 'dev'))
- grad_logit_w: float32 [2048], P(('tower', 'dev'))
All inputs are finite; a program needn't handle non-finite values.
Results may differ from a plain program's by a relative error of at most 0.025.
Values may be sent and summed in bfloat16 or wider, within the bound.
A program may use at most 128 MiB of HBM per device.

v0:
```python
import jax
import jax.numpy as jnp
from jax import lax
from jax.sharding import PartitionSpec as P

LOSS_SCALE = 1024


def inner_rows(left, right):
    return lax.dot_general(
        left, right, (((0,), (0,)), ((), ())), preferred_element_type=jnp.float32
    )


def outer_cols(left, right):
    return lax.dot_general(
        left, right, (((1,), (1,)), ((), ())), preferred_element_type=jnp.float32
    )


def silu_grad(values):
    sigmas = jax.nn.sigmoid(values)
    return sigmas * (1.0 + values * (1.0 - sigmas))


def local(
    embeddings,
    tower_v,
    tower_u,
    cross_bias,
    proj_w,
    proj_bias,
    arch_v,
    arch_u,
    arch_bias,
    logit_w,
    labels,
):
    towers = lax.axis_size("tower")
    members = lax.axis_size("dev")
    rows_all, own_cols = embeddings.shape
    sample_block = rows_all // (towers * members)
    folded = embeddings.reshape(towers, members, sample_block, own_cols)
    arrived = lax.all_to_all(folded, "dev", split_axis=1, concat_axis=3, tiled=True)
    width = own_cols * members
    base_rows = arrived.reshape(towers * sample_block, width)
    weight_v = tower_v[0]
    weight_u = tower_u[0]
    bias_c = cross_bias[0]
    weight_p = proj_w[0]
    bias_p = proj_bias[0]
    proj_width = weight_p.shape[1]
    low_rank = jnp.dot(base_rows, weight_v, preferred_element_type=jnp.float32).astype(jnp.bfloat16)
    crossed = jnp.dot(low_rank, weight_u, preferred_element_type=jnp.float32)
    base_f = base_rows.astype(jnp.float32)
    mixed = (base_f * (crossed + bias_c) + base_f).astype(jnp.bfloat16)
    pre_act = jnp.dot(mixed, weight_p, preferred_element_type=jnp.float32) + bias_p
    tower_out = jax.nn.silu(pre_act).astype(jnp.bfloat16)
    outgoing = tower_out.reshape(towers, sample_block, 1, proj_width)
    gathered = lax.all_to_all(outgoing, "tower", split_axis=0, concat_axis=2, tiled=True)
    arch_in = gathered.reshape(sample_block, towers * proj_width)
    arch_low = jnp.dot(arch_in, arch_v, preferred_element_type=jnp.float32).astype(jnp.bfloat16)
    arch_cross = jnp.dot(arch_low, arch_u, preferred_element_type=jnp.float32)
    arch_f = arch_in.astype(jnp.float32)
    arch_mix = (arch_f * (arch_cross + arch_bias) + arch_f).astype(jnp.bfloat16)
    mix_f = arch_mix.astype(jnp.float32)
    logits = jnp.sum(mix_f * logit_w, axis=1)
    grad_logits = (jax.nn.sigmoid(logits) - labels) * (LOSS_SCALE / rows_all)
    grad_logit_w = jnp.sum(grad_logits[:, None] * mix_f, axis=0)
    grad_mix = grad_logits[:, None] * logit_w[None, :]
    grad_arch_cross = grad_mix * arch_f
    grad_arch_bias = jnp.sum(grad_arch_cross, axis=0)
    grad_arch_cross_b = grad_arch_cross.astype(jnp.bfloat16)
    grad_arch_low = outer_cols(grad_arch_cross_b, arch_u).astype(jnp.bfloat16)
    grad_arch_in = (
        grad_mix * (arch_cross + arch_bias + 1.0) + outer_cols(grad_arch_low, arch_v)
    ).astype(jnp.bfloat16)
    grad_send = grad_arch_in.reshape(1, sample_block, towers, proj_width)
    grad_arch_u = inner_rows(arch_low, grad_arch_cross_b)
    grad_arch_v = inner_rows(arch_in, grad_arch_low)
    sum_av, sum_au, sum_ab, sum_lw = (
        lax.psum_scatter(grad_arch_v, ("tower", "dev"), scatter_dimension=0, tiled=True),
        lax.psum_scatter(grad_arch_u, ("tower", "dev"), scatter_dimension=0, tiled=True),
        lax.psum_scatter(grad_arch_bias, ("tower", "dev"), scatter_dimension=0, tiled=True),
        lax.psum_scatter(grad_logit_w, ("tower", "dev"), scatter_dimension=0, tiled=True),
    )
    back_out = lax.all_to_all(grad_send, "tower", split_axis=2, concat_axis=0, tiled=True)
    grad_out = back_out.reshape(towers * sample_block, proj_width)
    grad_pre = grad_out.astype(jnp.float32) * silu_grad(pre_act)
    grad_pbias = jnp.sum(grad_pre, axis=0)
    grad_pre_b = grad_pre.astype(jnp.bfloat16)
    grad_pw = inner_rows(mixed, grad_pre_b)
    grad_mixed = outer_cols(grad_pre_b, weight_p)
    grad_cross = grad_mixed * base_f
    grad_cbias = jnp.sum(grad_cross, axis=0)
    grad_cross_b = grad_cross.astype(jnp.bfloat16)
    grad_uw = inner_rows(low_rank, grad_cross_b)
    grad_low = outer_cols(grad_cross_b, weight_u).astype(jnp.bfloat16)
    grad_vw = inner_rows(base_rows, grad_low)
    grad_base = (grad_mixed * (crossed + bias_c + 1.0) + outer_cols(grad_low, weight_v)).astype(
        jnp.bfloat16
    )
    returning = grad_base.reshape(towers, 1, sample_block, width)
    landed = lax.all_to_all(returning, "dev", split_axis=3, concat_axis=1, tiled=True)
    emb_grad = landed.reshape(rows_all, own_cols)
    sum_vw, sum_uw, sum_cb, sum_pw, sum_pb = (
        lax.psum_scatter(
            grad_vw.astype(jnp.bfloat16), "dev", scatter_dimension=0, tiled=True
        ).astype(jnp.float32),
        lax.psum_scatter(
            grad_uw.astype(jnp.bfloat16), "dev", scatter_dimension=0, tiled=True
        ).astype(jnp.float32),
        lax.psum_scatter(
            grad_cbias.astype(jnp.bfloat16), "dev", scatter_dimension=0, tiled=True
        ).astype(jnp.float32),
        lax.psum_scatter(
            grad_pw.astype(jnp.bfloat16), "dev", scatter_dimension=0, tiled=True
        ).astype(jnp.float32),
        lax.psum_scatter(
            grad_pbias.astype(jnp.bfloat16), "dev", scatter_dimension=0, tiled=True
        ).astype(jnp.float32),
    )
    return (
        emb_grad,
        sum_vw[None],
        sum_uw[None],
        sum_cb[None],
        sum_pw[None],
        sum_pb[None],
        sum_av,
        sum_au,
        sum_ab,
        sum_lw,
    )


def solution(mesh):
    return jax.shard_map(
        local,
        mesh=mesh,
        in_specs=(
            P(None, ("tower", "dev")),
            P("tower", None, None),
            P("tower", None, None),
            P("tower", None),
            P("tower", None, None),
            P("tower", None),
            P(),
            P(),
            P(),
            P(),
            P(("tower", "dev")),
        ),
        out_specs=(
            P(None, ("tower", "dev")),
            P("tower", "dev", None),
            P("tower", "dev", None),
            P("tower", "dev"),
            P("tower", "dev", None),
            P("tower", "dev"),
            P(("tower", "dev"), None),
            P(("tower", "dev"), None),
            P(("tower", "dev")),
            P(("tower", "dev")),
        ),
        check_vma=False,
    )
```

profile of v0, /device:TPU:1, one launch (start us, length us, event | category | flops | bytes accessed | tf_op | source)
XLA Modules:
  0.0 995.6 jit_solution(16030671195492941314)
XLA Ops:
  8.1 2.6 copy.33
  10.7 56.6 %all_to_all.54 = bf16[16,8,64,256]{3,2,0,1:T(8,128)(2,1)S(1)} all-to-all(bf16[16,8,64,256]{3,2,0,1:T(8,128)(2,1)S(1)} %copy.33), channel_id=1, replica_groups=mesh['tower'=16,'dev'=8] {'dev'}, dimensions={1} | all-to-all | bytes 8388608 | tf_op jit(solution)/shard_map/all_to_all | solution.py:44
  67.3 2.9 copy.34
  70.2 1.5 copy.41
  71.8 1.2 convolution_convert_fusion.4
  73.7 4.8 fusion
  78.6 1.3 multiply_convert_fusion
  79.9 15.4 %all_to_all.55 = bf16[16,64,1,128]{3,1,2,0:T(8,128)(2,1)S(1)} all-to-all(bf16[16,64,1,128]{3,1,2,0:T(8,128)(2,1)S(1)} %bitcast.130), channel_id=1, replica_groups=mesh['tower'=16,'dev'=8] {'tower'}, dimensions={0} | all-to-all | bytes 524288 | tf_op jit(solution)/shard_map/all_to_all | solution.py:60
  98.8 10.6 %all_to_all.56 = bf16[1,64,16,128]{3,1,0,2:T(8,128)(2,1)S(1)} all-to-all(bf16[1,64,16,128]{3,1,0,2:T(8,128)(2,1)S(1)} %copy.37), channel_id=1, replica_groups=mesh['tower'=16,'dev'=8] {'tower'}, dimensions={2} | all-to-all | bytes 524288 | tf_op jit(solution)/shard_map/all_to_all | solution.py:87
  109.7 2.1 convolution_convert_fusion.2
  111.9 2.7 fusion.25
  114.8 3.6 fusion.1
  118.6 1.3 convolution_convert_fusion.3
  119.9 1.8 copy-done.4
  121.7 2.3 fusion.3
  124.1 7.1 convolution_convert_fusion
  131.3 2.7 fusion.18
  134.0 9.5 add_convert_fusion
  143.5 11.0 %copy.38 = bf16[16,1,64,2048]{2,0,1,3:T(8,128)(2,1)} copy(bf16[16,1,64,2048]{3,2,0,1:T(8,128)(2,1)} %bitcast.117) | data formatting | bytes 8388608 | tf_op jit(solution)/shard_map/reshape | solution.py:103
  154.5 10.5 %reshape.86 = bf16[8,2,131072]{2,1,0:T(2,128)(2,1)} reshape(bf16[2048,1,16,64]{3,2,1,0:T(8,128)(2,1)} %bitcast.115) | data formatting | bytes 8388608
  165.0 4.7 all-to-all-start.3
  172.0 104.3 %all-reduce.5 = (f32[2048]{0:T(1024)S(1)}, f32[2048]{0:T(1024)S(1)}) all-reduce(f32[2048]{0:T(1024)S(1)} %bitcast.134, f32[2048]{0:T(1024)S(1)} %fusion.12), channel_id=9, replica_groups=mesh['tower'=16,'dev'=8] {'tower','dev'}, use_global_device_ids=true, to_apply=%region_11.12.clone | all-reduce | flops 4096 | bytes 32768
  277.4 17.5 %all-reduce.6 = (bf16[2048]{0:T(1024)(128)(2,1)S(1)}, bf16[128]{0:T(256)(128)(2,1)S(1)}) all-reduce(bf16[2048]{0:T(1024)(128)(2,1)S(1)} %get-tuple-element.52, bf16[128]{0:T(256)(128)(2,1)S(1)} %get-tuple-element.44), channel_id=4, replica_groups=mesh['tower'=16,'dev'=8] {'dev'}, use_global_device_ids=true, to_apply=%region_4.5.clone | all-reduce | flops 2176 | bytes 8704
  296.2 1.5 bitcast_convert_fusion.3
  297.7 3.4 all-reduce.9.cloned.1.call-done
  301.1 1.5 constant_dynamic-slice_fusion
  302.5 0.9 bitcast_convert_fusion.2
  304.3 51.7 %reduce-scatter.7.cloned.1.call-done = bf16[32,2048]{1,0:T(8,128)(2,1)} async-done(((bf16[256,2048]{1,0:T(8,128)(2,1)}), bf16[32,2048]{1,0:T(8,128)(2,1)}) %reduce-scatter.7.cloned.1.call-update) | async-done | bytes 131088 | tf_op jit(solution)/shard_map/reduce_scatter | solution.py:110
  356.0 1.6 bitcast_convert_fusion.1
  357.7 10.3 %reshape.87 = bf16[2048,1,16,64]{3,2,1,0:T(8,128)(2,1)} reshape(bf16[8,2,131072]{2,1,0:T(2,128)(2,1)} %all-to-all-done.3) | data formatting | bytes 8388608
  368.0 9.9 copy.39
  377.9 610.5 %reduce-scatter.11.cloned.1.call-done = f32[16,512]{1,0:T(8,128)} async-done(((f32[2048,512]{1,0:T(8,128)}), f32[16,512]{1,0:T(8,128)}) %reduce-scatter.11.cloned.1.call-update) | async-done | bytes 32784 | tf_op jit(solution)/shard_map/reduce_scatter | solution.py:82
  (74 shorter events, 9.1 us)
Async XLA Ops:
  8.0 88.4 %copy-start = (bf16[512,2048]{1,0:T(8,128)(2,1)S(1)}, bf16[512,2048]{1,0:T(8,128)(2,1)}, u32[]{:S(2)}) copy-start(bf16[512,2048]{1,0:T(8,128)(2,1)} %param.18) | copy-start | bytes 6291460
  8.0 288.1 %reduce-scatter.9.cloned.1.call-start = ((), (), s32[]{:S(2)}) async-start(), calls=%async_computation.10 | async-start | bytes 589824 | tf_op jit(solution)/shard_map/reduce_scatter | solution.py:116
  70.2 1.5 copy-start.10
  71.7 6.8 copy-start.2
  71.7 2.0 copy-start.6
  71.7 2.0 copy-start.15
  73.7 4.8 copy-start.12
  73.7 4.8 copy-start.19
  78.6 17.4 %copy-start.5 = (bf16[2048,512]{1,0:T(8,128)(2,1)S(1)}, bf16[2048,512]{1,0:T(8,128)(2,1)}, u32[]{:S(2)}) copy-start(bf16[2048,512]{1,0:T(8,128)(2,1)} %param.17) | copy-start | bytes 6291460
  78.6 17.9 %copy-start.14 = (f32[2048]{0:T(1024)S(1)}, f32[2048]{0:T(1024)}, u32[]{:S(2)}) copy-start(f32[2048]{0:T(1024)} %param.20) | copy-start | bytes 24580
  78.6 17.9 %copy-start.18 = (f32[2048]{0:T(1024)S(1)}, f32[2048]{0:T(1024)}, u32[]{:S(2)}) copy-start(f32[2048]{0:T(1024)} %param.19) | copy-start | bytes 24580
  79.9 17.2 %copy-start.20 = (f32[64]{0:T(128)S(1)}, f32[64]{0:T(128)}, u32[]{:S(2)}) copy-start(f32[64]{0:T(128)} %param.21) | copy-start | bytes 772
  95.3 0.7 copy-start.8
  97.1 12.6 %copy-start.16 = (f32[64]{0:T(128)}, f32[64]{0:T(128)S(1)}, u32[]{:S(2)}) copy-start(f32[64]{0:T(128)S(1)} %fusion.28) | copy-start | bytes 772
  109.7 2.2 copy-start.17
  111.9 2.9 copy-start.13
  111.9 189.2 %all-reduce.9.cloned.1.call-start = ((), (), s32[]{:S(2)}) async-start(), calls=%async_computation.12 | async-start | bytes 8388608
  114.7 3.7 copy-start.7
  114.7 187.8 %reduce-scatter.5.cloned.1.call-start = ((), (), s32[]{:S(2)}) async-start(), calls=%async_computation.8 | async-start | bytes 1179648 | tf_op jit(solution)/shard_map/reduce_scatter | solution.py:107
  114.8 3.8 copy-start.3
  118.4 3.2 copy-start.4
  124.0 232.0 %reduce-scatter.7.cloned.1.call-start = ((), (), s32[]{:S(2)}) async-start(), calls=%async_computation.9 | async-start | bytes 1179648 | tf_op jit(solution)/shard_map/reduce_scatter | solution.py:110
  131.2 2.8 copy-start.11
  131.2 857.2 %reduce-scatter.11.cloned.1.call-start = ((), (), s32[]{:S(2)}) async-start(), calls=%async_computation.11 | async-start | bytes 4227072 | tf_op jit(solution)/shard_map/reduce_scatter | solution.py:82
  165.0 4.8 copy-start.21
  165.0 6.6 copy-start.9
  165.0 192.7 %all-to-all-start.3 = ((bf16[8,2,131072]{2,1,0:T(2,128)(2,1)}), bf16[8,2,131072]{2,1,0:T(2,128)(2,1)}, u32[]{:S(2)}, u32[]{:S(2)}) async-start(bf16[8,2,131072]{2,1,0:T(2,128)(2,1)} %reshape.86), calls=%async_computation.3 | async-start | bytes 8388608 | tf_op jit(solution)/shard_map/all_to_all | solution.py:104
  368.0 620.4 %copy-start.1 = (bf16[512,2048]{1,0:T(8,128)(2,1)S(1)}, bf16[512,2048]{1,0:T(8,128)(2,1)}, u32[]{:S(2)}) copy-start(bf16[512,2048]{1,0:T(8,128)(2,1)} %param.18) | copy-start | bytes 6291460
Sparse Core Ops, SparseCore 0:
  112.0 80.4 reduce-scatter.8
  196.5 85.5 reduce-scatter.4
  285.7 70.2 reduce-scatter.6
  358.9 629.4 reduce-scatter.10
Sparse Core Ops, SparseCore 1:
  117.3 183.7 all-reduce.8
where the time goes:
time: 1010 us; the launch traced here: 996 us
  waiting for transfers between devices  666 us (66%)
  blocking collectives  204 us (20%)
  local copies, waits for them, and re-layouts  56.3 us (6%)
  matrix products  41.4 us (4%)
  between operations  16.9 us (2%)
    reduce_scatter x1, waiting for transfers between devices, local(): lax.psum_scatter(grad_arch_v, ('tower', 'dev'), scatter_dimension=0, tile...  610 us
    unnamed x2, blocking collectives  122 us
    all_to_all x1, blocking collectives, local(): lax.all_to_all(folded, 'dev', split_axis=1, concat_axis=3, tiled=True)  56.6 us
    reduce_scatter x1, waiting for transfers between devices, local(): lax.psum_scatter(grad_uw.astype(jnp.bfloat16), 'dev', scatter_dimension=0...  51.7 us
    unnamed x53, local copies, waits for them, and re-layouts  29.7 us
  transfers between devices with their start and end apart: 6, of which 3 were waited for; matrix products, arithmetic and copies ran while one was open for 8% of the time, Pallas kernels for 0%

commit v1 on v0

v1 whole, which is shorter than its diff:
```python
import functools

import jax
import jax.numpy as jnp
from jax import lax
from jax.experimental import pallas as pl
from jax.experimental.pallas import tpu as pltpu
from jax.sharding import PartitionSpec as P

LOSS_SCALE = 1024
NC = 2
F32 = jnp.float32
BF16 = jnp.bfloat16
MESH = pl.DeviceIdType.MESH


def dot(a, b):
    return jnp.dot(a, b, preferred_element_type=F32)


def dot_t(a, b):
    return lax.dot_general(a, b, (((1,), (1,)), ((), ())), preferred_element_type=F32)


def kernel(
    dims,
    emb, tv_h, tu_h, cb, pw_h, pb, av_h, au_h, ab, lw, labels,
    emb_out, vw_out, uw_out, cb_out, pw_out, pb_out, gav_out, gau_out, gab_out, glw_out,
    base, tv, tu, pw, av, au,
    low, scale, mixed, sgrad, gpre, gcb, glow,
    out, arch_in, back_s, back_r, ag, eg,
    vw_acc, uw_acc, pw_acc, cb_acc, pb_acc, vec_acc,
    w_s, w_r, u_s, u_r, a1_s, a1_r, a2_s, a2_r,
    local_sem, fwd_ss, fwd_rs, out_ss, out_rs, back_ss, back_rs, ag_ss, ag_rs,
    emb_ss, emb_rs, w_ss, w_rs, u_ss, u_rs, a1_ss, a1_rs, a2_ss, a2_rs,
):
    T, D, SB, OC = dims["T"], dims["D"], dims["SB"], dims["OC"]
    HI = 2
    DY = D // HI
    SC = SB // NC
    R = T * SC
    W = D * OC
    RANK, PROJ, AR = dims["RANK"], dims["PROJ"], dims["AR"]
    ARCH = T * PROJ
    RR = RANK // D
    AP = PROJ // D
    UR = AR // T
    UF = UR // D
    t = lax.axis_index("tower")
    d = lax.axis_index("dev")
    d_hi = lax.div(d, DY)
    d_y = lax.rem(d, DY)

    def dev(k):
        hi = lax.rem(d_hi + lax.div(k, DY), HI)
        return hi * DY + lax.rem(d_y + lax.rem(k, DY), DY)

    def tow(k):
        return lax.rem(t + k, T)

    def cols(j, n):
        return pl.ds(pl.multiple_of(j * n, n), n)

    def loop(lo, hi, f):
        lax.fori_loop(lo, hi, lambda i, x: (f(i), x)[1], 0)

    def remote(src, dst, ss, rs, who):
        return pltpu.make_async_remote_copy(
            src_ref=src, dst_ref=dst, send_sem=ss, recv_sem=rs, device_id=who, device_id_type=MESH
        )

    barrier = pltpu.get_barrier_semaphore()
    loop(1, D, lambda k: pl.semaphore_signal(
        barrier, inc=1, device_id=(t, dev(jnp.int32(k))), device_id_type=MESH))
    loop(1, T, lambda k: pl.semaphore_signal(
        barrier, inc=1, device_id=(tow(k), d), device_id_type=MESH))
    pl.semaphore_wait(barrier, D + T - 2)

    def fwd(c, k):
        j = dev(k)
        return remote(
            emb.at[:, j, pl.ds(c * SC, SC), :], base.at[c, :, :, cols(d, OC)],
            fwd_ss.at[c, k], fwd_rs.at[c, d], (t, j))

    def fwd_arrival(c, k):
        j = dev(k)
        return remote(
            emb.at[:, j, pl.ds(c * SC, SC), :], base.at[c, :, :, cols(j, OC)],
            fwd_ss.at[c, k], fwd_rs.at[c, j], (t, j))

    def tower_out(c, k):
        j = tow(k)
        return remote(
            out.at[c, j], arch_in.at[c, :, cols(t, PROJ)],
            out_ss.at[c, k], out_rs.at[c, t], (j, d))

    def tower_out_arrival(c, k):
        j = tow(k)
        return remote(
            out.at[c, j], arch_in.at[c, :, cols(j, PROJ)],
            out_ss.at[c, k], out_rs.at[c, j], (j, d))

    def back(c, k, who):
        j = tow(k)
        return remote(
            back_s.at[c, j], back_r.at[c, who], back_ss.at[c, k], back_rs.at[c, who], (j, d))

    def gather(c, k, who):
        j = tow(k)
        return remote(ag.at[c, t], ag.at[c, who], ag_ss.at[c, k], ag_rs.at[c, who], (j, d))

    def emb_back(c, k, who):
        j = dev(k)
        return remote(
            eg.at[c, j], emb_out.at[:, who, pl.ds(c * SC, SC), :],
            emb_ss.at[c, k], emb_rs.at[c, who], (t, j))

    def over_dev(s, r, ss, rs):
        def make(k, who):
            j = dev(k)
            return remote(s.at[j], r.at[who], ss.at[k], rs.at[who], (t, j))
        return make

    w_copy = over_dev(w_s, w_r, w_ss, w_rs)
    u_copy = over_dev(u_s, u_r, u_ss, u_rs)
    a2_copy = over_dev(a2_s, a2_r, a2_ss, a2_rs)

    def a1_copy(k, who):
        j = tow(k)
        return remote(a1_s.at[j], a1_r.at[who], a1_ss.at[k], a1_rs.at[who], (j, d))

    def fwd_own(c):
        return pltpu.make_async_copy(
            emb.at[:, d, pl.ds(c * SC, SC), :], base.at[c, :, :, cols(d, OC)], local_sem.at[c])

    def emb_own(c):
        return pltpu.make_async_copy(
            eg.at[c, d], emb_out.at[:, d, pl.ds(c * SC, SC), :], local_sem.at[NC + c])

    weights = [
        pltpu.make_async_copy(src, dst, local_sem.at[2 * NC + i])
        for i, (src, dst) in enumerate(
            [(tv_h, tv), (tu_h, tu), (pw_h, pw), (av_h, av), (au_h, au)])
    ]

    def start_fwd(c):
        loop(1, D, lambda k: fwd(c, k).start())

    for c in range(NC):
        start_fwd(c)
    for w in weights:
        w.start()
    for c in range(NC):
        fwd_own(c).start()

    vw_acc[...] = jnp.zeros_like(vw_acc)
    uw_acc[...] = jnp.zeros_like(uw_acc)
    pw_acc[...] = jnp.zeros_like(pw_acc)
    cb_acc[...] = jnp.zeros_like(cb_acc)
    pb_acc[...] = jnp.zeros_like(pb_acc)
    vec_acc[...] = jnp.zeros_like(vec_acc)
    for w in weights:
        w.wait()

    def chunk(c):
        fwd_own(c).wait()
        loop(1, D, lambda k: fwd_arrival(c, k).wait_recv())
        low[...] = dot(base[c].reshape(R, W), tv[...]).astype(BF16)

        def forward_cols(j):
            at = cols(j, OC)
            s = dot(low[...], tu[:, at]) + (cb[:, at] + 1.0)
            scale[:, at] = s
            b = base[c, :, :, at].reshape(R, OC).astype(F32)
            mixed[:, at] = (b * s).astype(BF16)

        loop(0, D, forward_cols)
        pre = dot(mixed[...], pw[...]) + pb[...]
        sig = jax.nn.sigmoid(pre)
        sgrad[...] = sig * (1.0 + pre * (1.0 - sig))
        out[c] = (pre * sig).astype(BF16).reshape(T, SC, PROJ)
        loop(1, T, lambda k: tower_out(c, k).start())
        arch_in[c, :, cols(t, PROJ)] = out[c, t]
        loop(1, T, lambda k: tower_out_arrival(c, k).wait_recv())

        a_in = arch_in[c]
        a_low = dot(a_in, av[...]).astype(BF16)
        a_scale = dot(a_low, au[...]) + (ab[...] + 1.0)
        a_f = a_in.astype(F32)
        mix = (a_f * a_scale).astype(BF16).astype(F32)
        logits = jnp.sum(mix * lw[...], axis=1, keepdims=True)
        row = lax.broadcasted_iota(jnp.int32, (SC, SB), 0) + c * SC
        lane = lax.broadcasted_iota(jnp.int32, (SC, SB), 1)
        label = jnp.sum(
            jnp.where(row == lane, jnp.broadcast_to(labels[...], (SC, SB)), 0.0),
            axis=1, keepdims=True)
        g = (jax.nn.sigmoid(logits) - label) * (LOSS_SCALE / (T * D * SB))
        vec_acc[1:2, :] += jnp.sum(g * mix, axis=0, keepdims=True)
        g_mix = g * lw[...]
        g_cross = g_mix * a_f
        vec_acc[0:1, :] += jnp.sum(g_cross, axis=0, keepdims=True)
        g_cross_b = g_cross.astype(BF16)
        g_low = dot_t(g_cross_b, au[...]).astype(BF16)
        g_in = (g_mix * a_scale + dot_t(g_low, av[...])).astype(BF16)
        for j in range(T):
            back_s[c, j, :, 0:PROJ] = g_in[:, j * PROJ:(j + 1) * PROJ]
            back_s[c, j, :, PROJ:2 * PROJ] = g_cross_b[:, j * PROJ:(j + 1) * PROJ]
        loop(1, T, lambda k: back(c, k, t).start())
        back_r[c, t] = back_s[c, t]
        ag[c, t, :, 0:AR] = a_low
        ag[c, t, :, AR:2 * AR] = g_low
        loop(1, T, lambda k: gather(c, k, t).start())

        loop(1, T, lambda k: back(c, k, tow(k)).wait_recv())
        g_pre = back_r[c, :, :, 0:PROJ].reshape(R, PROJ).astype(F32) * sgrad[...]
        pb_acc[...] += jnp.sum(g_pre, axis=0, keepdims=True)
        gpre[...] = g_pre.astype(BF16)

        def backward_cols(j):
            at = cols(j, OC)
            gm = dot_t(gpre[...], pw[at, :])
            gc = gm * base[c, :, :, at].reshape(R, OC).astype(F32)
            cb_acc[:, at] += jnp.sum(gc, axis=0, keepdims=True)
            gcb[:, at] = gc.astype(BF16)
            scale[:, at] = gm * scale[:, at]

        loop(0, D, backward_cols)
        glow[...] = dot_t(gcb[...], tu[...]).astype(BF16)

        def grad_cols(j):
            at = cols(j, OC)
            v = scale[:, at] + dot_t(glow[...], tv[at, :])
            eg[c, j] = v.astype(BF16).reshape(T, SC, OC)

        def grad_send(k):
            grad_cols(dev(k))
            emb_back(c, k, d).start()

        loop(1, D, grad_send)
        grad_cols(d)
        emb_own(c).start()

        glow_t = glow[...].T
        low_t = low[...].T
        gpre_t = gpre[...].T

        def weight_cols(j):
            at = cols(j, OC)
            vw_acc[:, at] += dot(glow_t, base[c, :, :, at].reshape(R, OC))
            uw_acc[:, at] += dot(low_t, gcb[:, at])
            pw_acc[:, at] += dot(gpre_t, mixed[:, at])

        loop(0, D, weight_cols)

    loop(0, NC, chunk)

    for c in range(NC):
        loop(1, T, lambda k: gather(c, k, tow(k)).wait_recv())
    gathered = ag[...].reshape(NC * R, 2 * AR)
    gav = dot(out[...].reshape(NC * R, PROJ).T, gathered[:, AR:])
    gau = dot(back_r[:, :, :, PROJ:].reshape(NC * R, PROJ).T, gathered[:, :AR]).T
    for j in range(T):
        a1_s[j, 0:UR, :] = gau[j * UR:(j + 1) * UR, :]
        a1_s[j, UR:UR + 8, :] = vec_acc[:, j * PROJ:(j + 1) * PROJ]
    loop(1, T, lambda k: a1_copy(k, t).start())
    a1_r[t] = a1_s[t]
    half = ARCH // 2
    for j in range(D):
        a2_s[j, 8:16, 0:AR] = gav[j * AP:j * AP + 8, :]
        a2_s[j, 8:16, AR:2 * AR] = gav[j * AP + 8:j * AP + 16, :]

    for j in range(D):
        at = slice(j * OC, (j + 1) * OC)
        u_s[j] = uw_acc[j * RR:(j + 1) * RR, :].astype(BF16)
        w_s[j, 0:RANK, :] = vw_acc[:, at].astype(BF16)
        w_s[j, RANK:RANK + PROJ, :] = pw_acc[:, at].astype(BF16)
        first = lax.broadcasted_iota(jnp.int32, (16, OC), 0) == 0
        pb2 = jnp.concatenate([pb_acc[...]] * (OC // PROJ), axis=1)
        w_s[j, RANK + PROJ:RANK + PROJ + 16, :] = jnp.where(
            first, jnp.broadcast_to(cb_acc[:, at], (16, OC)), jnp.broadcast_to(pb2, (16, OC))
        ).astype(BF16)

    def send_weights(k):
        u_copy(k, d).start()
        w_copy(k, d).start()

    loop(1, D, send_weights)
    u_r[d] = u_s[d]
    w_r[d] = w_s[d]

    loop(1, T, lambda k: a1_copy(k, tow(k)).wait_recv())
    vec = jnp.sum(a1_r[:, UR:UR + 8, :], axis=0)
    per = half // PROJ
    for j in range(D):
        for i in range(T):
            r0 = UF * (i // per)
            c0 = (i % per) * PROJ
            a2_s[j, r0:r0 + UF, c0:c0 + PROJ] = a1_r[i, j * UF:(j + 1) * UF, :]
        a2_s[j, 0:8, half:half + PROJ] = vec
        a2_s[j, 8:16, half:half + PROJ] = vec
    loop(1, D, lambda k: a2_copy(k, d).start())
    a2_r[d] = a2_s[d]

    loop(1, D, lambda k: a2_copy(k, dev(k)).wait_recv())
    a2 = jnp.sum(a2_r[...], axis=0)
    gau_out[:, 0:half] = a2[0:UF, 0:half]
    gau_out[:, half:] = a2[UF:2 * UF, 0:half]
    gav_out[0:8, :] = a2[8:16, 0:AR]
    gav_out[8:16, :] = a2[8:16, AR:2 * AR]
    shift = lax.rem(PROJ - d * AP, PROJ)
    vec = pltpu.roll(a2[0:8, half:half + PROJ], shift, 1)
    gab_out[...] = vec[0:1, 0:AP]
    glw_out[...] = vec[1:2, 0:AP]

    loop(1, D, lambda k: u_copy(k, dev(k)).wait_recv())
    loop(1, D, lambda k: w_copy(k, dev(k)).wait_recv())
    uw_out[...] = jnp.sum(u_r[...].astype(F32), axis=0)
    ws = jnp.sum(w_r[...].astype(F32), axis=0)
    vw_out[...] = ws[0:RANK].T
    pw_out[...] = ws[RANK:RANK + PROJ].T
    cb_out[...] = ws[RANK + PROJ:RANK + PROJ + 1]
    vec = pltpu.roll(ws[RANK + PROJ + 8:RANK + PROJ + 16, 0:PROJ], shift, 1)
    pb_out[...] = vec[0:1, 0:AP]

    for c in range(NC):
        emb_own(c).wait()

        def drain_dev(k):
            fwd(c, k).wait_send()
            emb_back(c, k, d).wait_send()
            emb_back(c, k, dev(k)).wait_recv()

        def drain_tower(k):
            tower_out(c, k).wait_send()
            back(c, k, t).wait_send()
            gather(c, k, t).wait_send()

        loop(1, D, drain_dev)
        loop(1, T, drain_tower)

    def drain_last(k):
        u_copy(k, d).wait_send()
        w_copy(k, d).wait_send()
        a2_copy(k, d).wait_send()

    loop(1, D, drain_last)
    loop(1, T, lambda k: a1_copy(k, t).wait_send())


def local(
    embeddings, tower_v, tower_u, cross_bias, proj_w, proj_bias,
    arch_v, arch_u, arch_bias, logit_w, labels,
):
    T = lax.axis_size("tower")
    D = lax.axis_size("dev")
    rows, OC = embeddings.shape
    SB = rows // (T * D)
    SC = SB // NC
    R = T * SC
    W = D * OC
    RANK = tower_v.shape[2]
    PROJ = proj_w.shape[2]
    ARCH, AR = arch_v.shape
    UR = AR // T
    AP = PROJ // D
    WR = RANK + PROJ + 16
    A2 = ARCH // 2 + PROJ
    dims = dict(T=T, D=D, SB=SB, OC=OC, RANK=RANK, PROJ=PROJ, AR=AR)
    vmem = pl.BlockSpec(memory_space=pltpu.VMEM)
    hbm = pl.BlockSpec(memory_space=pl.ANY)
    dma = pltpu.SemaphoreType.DMA
    outs = pl.pallas_call(
        functools.partial(kernel, dims),
        out_shape=(
            jax.ShapeDtypeStruct((T, D, SB, OC), BF16),
            jax.ShapeDtypeStruct((W // D, RANK), F32),
            jax.ShapeDtypeStruct((RANK // D, W), F32),
            jax.ShapeDtypeStruct((1, OC), F32),
            jax.ShapeDtypeStruct((W // D, PROJ), F32),
            jax.ShapeDtypeStruct((1, AP), F32),
            jax.ShapeDtypeStruct((AP, AR), F32),
            jax.ShapeDtypeStruct((UR // D, ARCH), F32),
            jax.ShapeDtypeStruct((1, AP), F32),
            jax.ShapeDtypeStruct((1, AP), F32),
        ),
        in_specs=[hbm, hbm, hbm, vmem, hbm, vmem, hbm, hbm, vmem, vmem, vmem],
        out_specs=(hbm,) + (vmem,) * 9,
        scratch_shapes=[
            pltpu.VMEM((NC, T, SC, W), BF16),
            pltpu.VMEM((W, RANK), BF16),
            pltpu.VMEM((RANK, W), BF16),
            pltpu.VMEM((W, PROJ), BF16),
            pltpu.VMEM((ARCH, AR), BF16),
            pltpu.VMEM((AR, ARCH), BF16),
            pltpu.VMEM((R, RANK), BF16),
            pltpu.VMEM((R, W), F32),
            pltpu.VMEM((R, W), BF16),
            pltpu.VMEM((R, PROJ), F32),
            pltpu.VMEM((R, PROJ), BF16),
            pltpu.VMEM((R, W), BF16),
            pltpu.VMEM((R, RANK), BF16),
            pltpu.VMEM((NC, T, SC, PROJ), BF16),
            pltpu.VMEM((NC, SC, ARCH), BF16),
            pltpu.VMEM((NC, T, SC, 2 * PROJ), BF16),
            pltpu.VMEM((NC, T, SC, 2 * PROJ), BF16),
            pltpu.VMEM((NC, T, SC, 2 * AR), BF16),
            pltpu.VMEM((NC, D, T, SC, OC), BF16),
            pltpu.VMEM((RANK, W), F32),
            pltpu.VMEM((RANK, W), F32),
            pltpu.VMEM((PROJ, W), F32),
            pltpu.VMEM((1, W), F32),
            pltpu.VMEM((1, PROJ), F32),
            pltpu.VMEM((8, ARCH), F32),
            pltpu.VMEM((D, WR, OC), BF16),
            pltpu.VMEM((D, WR, OC), BF16),
            pltpu.VMEM((D, RANK // D, W), BF16),
            pltpu.VMEM((D, RANK // D, W), BF16),
            pltpu.VMEM((T, UR + 8, PROJ), F32),
            pltpu.VMEM((T, UR + 8, PROJ), F32),
            pltpu.VMEM((D, 16, A2), F32),
            pltpu.VMEM((D, 16, A2), F32),
            dma((2 * NC + 5,)),
            dma((NC, D)), dma((NC, D)),
            dma((NC, T)), dma((NC, T)),
            dma((NC, T)), dma((NC, T)),
            dma((NC, T)), dma((NC, T)),
            dma((NC, D)), dma((NC, D)),
            dma((D,)), dma((D,)),
            dma((D,)), dma((D,)),
            dma((T,)), dma((T,)),
            dma((D,)), dma((D,)),
        ],
        compiler_params=pltpu.CompilerParams(
            collective_id=0, has_side_effects=True, vmem_limit_bytes=60 << 20
        ),
    )(
        embeddings.reshape(T, D, SB, OC), tower_v[0], tower_u[0], cross_bias, proj_w[0], proj_bias,
        arch_v, arch_u, arch_bias[None], logit_w[None], labels[None],
    )
    eg, vw, uw, cb, pw, pb, gav, gau, gab, glw = outs
    return (
        eg.reshape(rows, OC), vw[None], uw[None], cb, pw[None], pb,
        gav, gau, gab[0], glw[0],
    )


def solution(mesh):
    return jax.shard_map(
        local,
        mesh=mesh,
        in_specs=(
            P(None, ("tower", "dev")),
            P("tower", None, None),
            P("tower", None, None),
            P("tower", None),
            P("tower", None, None),
            P("tower", None),
            P(),
            P(),
            P(),
            P(),
            P(("tower", "dev")),
        ),
        out_specs=(
            P(None, ("tower", "dev")),
            P("tower", "dev", None),
            P("tower", "dev", None),
            P("tower", "dev"),
            P("tower", "dev", None),
            P("tower", "dev"),
            P(("tower", "dev"), None),
            P(("tower", "dev"), None),
            P(("tower", "dev")),
            P(("tower", "dev")),
        ),
        check_vma=False,
    )
```

time: 1010 us -> 202 us (0.20); the launches traced: 996 us -> 202 us
  waiting for transfers between devices: 666 us -> 0 us
  blocking collectives: 204 us -> 0 us
  Pallas kernels: 0 us -> 191 us
  local copies, waits for them, and re-layouts: 56.3 us -> 9.94 us
  matrix products: 41.4 us -> 0 us
  between operations: 16.9 us -> 0.74 us
    reduce_scatter x4 -> x0, waiting for transfers between devices: 662 us -> none  [the longest x1 610 us: local(): lax.psum_scatter(grad_arch_v, ('tower', 'dev'), scatter_dimension=0, tile...]
    pallas_call x0 -> x1, Pallas kernels: none -> 191 us  [local(): pl.pallas_call(functools.partial(kernel, dims), out_shape=(jax.ShapeDtype...]
    unnamed x2 -> x0, blocking collectives: 122 us -> none
    all_to_all x3 -> x0, blocking collectives: 82.6 us -> none  [the longest x1 56.6 us: local(): lax.all_to_all(folded, 'dev', split_axis=1, concat_axis=3, tiled=True)]
    dot_general x15 -> x0, matrix products: 41.4 us -> none  [the longest x5 17 us: inner_rows(): lax.dot_general(left, right, (((0,), (0,)), ((), ())), preferred_element_...]
    unnamed x53 -> x28, local copies, waits for them, and re-layouts: 29.7 us -> 9.94 us
    reshape x3 -> x0, local copies, waits for them, and re-layouts: 13.7 us -> none  [the longest x1 11 us: local(): returning = grad_base.reshape(towers, 1, sample_block, width)]
    all_to_all x3 -> x0, local copies, waits for them, and re-layouts: 13 us -> none  [the longest x1 9.9 us: local(): lax.all_to_all(returning, 'dev', split_axis=3, concat_axis=1, tiled=True)]
  transfers between devices with their start and end apart: 6 -> 0, of which waited for: 3 -> 0; matrix products, arithmetic and copies ran while one was open for 8% -> 0% of each run, Pallas kernels for 0% -> 0%
where the time goes in v1:
time: 202 us
  Pallas kernels  191 us (95%)
  local copies, waits for them, and re-layouts  9.94 us (5%)
    pallas_call x1, Pallas kernels, local(): pl.pallas_call(functools.partial(kernel, dims), out_shape=(jax.ShapeDtype...  191 us
    unnamed x28, local copies, waits for them, and re-layouts  9.94 us

profile of v1, /device:TPU:1, one launch (start us, length us, event | category | flops | bytes accessed | tf_op | source)
XLA Modules:
  0.0 202.0 jit_solution(10577699714113381734)
XLA Ops:
  0.6 191.3 %shard_map.186 = (bf16[16,8,64,256]{3,2,1,0:T(8,128)(2,1)}, f32[256,256]{1,0:T(8,128)}, f32[32,2048]{1,0:T(8,128)}, f32[1,256]{1,0:T(1,128)}, f32[256,128]{1,0:T...) custom-call(bf16[16,8,64,256]{3,2,1,0:T(8,128)(2,1)} %bitcast.13, ...), custom_call_target="tpu_custom_call" | custom-call | tf_op jit(solution)/shard_map/pallas_call | solution.py:372
  192.0 0.0 copy-start.1
  192.0 0.0 copy-start
  192.0 0.0 copy-start.5
  192.0 0.0 copy-start.2
  192.0 0.0 copy-start.8
  192.0 0.0 copy-start.4
  192.0 0.0 copy-start.3
  192.0 0.0 copy-start.7
  192.0 0.0 copy-start.6
  192.0 4.5 %copy.31 = bf16[8192,256]{1,0:T(8,128)(2,1)} copy(bf16[8192,256]{1,0:T(8,128)(2,1)} %bitcast.14) | data formatting | bytes 8388608
  196.6 0.0 copy-done.1
  196.6 0.7 copy.32
  197.3 0.0 copy-done
  197.3 0.7 copy.33
  198.0 0.0 copy-done.5
  198.0 0.6 copy.34
  198.5 0.0 copy-done.2
  198.5 0.7 copy.35
  199.2 0.0 copy-done.8
  199.2 0.5 copy.36
  199.7 0.0 copy-done.4
  199.7 0.6 copy.37
  200.3 0.0 copy-done.3
  200.3 0.6 copy.38
  200.9 0.0 copy-done.7
  200.9 0.5 copy.39
  201.5 0.0 copy-done.6
  201.5 0.5 copy.40
Async XLA Ops:
  192.0 4.6 %copy-start.1 = (f32[256,256]{1,0:T(8,128)S(1)}, f32[256,256]{1,0:T(8,128)}, u32[]{:S(2)}) copy-start(f32[256,256]{1,0:T(8,128)} %get-tuple-element.21) | copy-start | bytes 786436
  192.0 5.3 %copy-start = (f32[32,2048]{1,0:T(8,128)S(1)}, f32[32,2048]{1,0:T(8,128)}, u32[]{:S(2)}) copy-start(f32[32,2048]{1,0:T(8,128)} %get-tuple-element.22) | copy-start | bytes 786436
  192.0 6.0 %copy-start.5 = (f32[1,256]{1,0:T(1,128)S(1)}, f32[1,256]{1,0:T(1,128)}, u32[]{:S(2)}) copy-start(f32[1,256]{1,0:T(1,128)} %get-tuple-element.43) | copy-start | bytes 3076
  192.0 6.6 %copy-start.2 = (f32[256,128]{1,0:T(8,128)S(1)}, f32[256,128]{1,0:T(8,128)}, u32[]{:S(2)}) copy-start(f32[256,128]{1,0:T(8,128)} %get-tuple-element.24) | copy-start | bytes 393220
  192.0 7.2 %copy-start.8 = (f32[1,16]{1,0:T(1,128)S(1)}, f32[1,16]{1,0:T(1,128)}, u32[]{:S(2)}) copy-start(f32[1,16]{1,0:T(1,128)} %get-tuple-element.45) | copy-start | bytes 196
  192.0 7.7 %copy-start.4 = (f32[16,512]{1,0:T(8,128)S(1)}, f32[16,512]{1,0:T(8,128)}, u32[]{:S(2)}) copy-start(f32[16,512]{1,0:T(8,128)} %get-tuple-element.46) | copy-start | bytes 98308
  192.0 8.3 %copy-start.3 = (f32[4,2048]{1,0:T(4,128)S(1)}, f32[4,2048]{1,0:T(4,128)}, u32[]{:S(2)}) copy-start(f32[4,2048]{1,0:T(4,128)} %get-tuple-element.47) | copy-start | bytes 98308
  192.0 8.9 %copy-start.7 = (f32[1,16]{1,0:T(1,128)S(1)}, f32[1,16]{1,0:T(1,128)}, u32[]{:S(2)}) copy-start(f32[1,16]{1,0:T(1,128)} %get-tuple-element.28) | copy-start | bytes 196
  192.0 9.4 %copy-start.6 = (f32[1,16]{1,0:T(1,128)S(1)}, f32[1,16]{1,0:T(1,128)}, u32[]{:S(2)}) copy-start(f32[1,16]{1,0:T(1,128)} %get-tuple-element.29) | copy-start | bytes 196

commit v2 on v1

--- a/solution.py
+++ b/solution.py
@@ -8,7 +8,7 @@
 from jax.sharding import PartitionSpec as P
 
 LOSS_SCALE = 1024
-NC = 2
+NC = 4
 F32 = jnp.float32
 BF16 = jnp.bfloat16
 MESH = pl.DeviceIdType.MESH
@@ -25,13 +25,14 @@
 def kernel(
     dims,
     emb, tv_h, tu_h, cb, pw_h, pb, av_h, au_h, ab, lw, labels,
-    emb_out, vw_out, uw_out, cb_out, pw_out, pb_out, gav_out, gau_out, gab_out, glw_out,
+    emb_land, vw_out, uw_out, cb_out, pw_out, pb_out, gav_out, gau_out, gab_out, glw_out,
     base, tv, tu, pw, av, au,
     low, scale, mixed, sgrad, gpre, gcb, glow,
     out, arch_in, back_s, back_r, ag, eg,
-    vw_acc, uw_acc, pw_acc, cb_acc, pb_acc, vec_acc,
-    w_s, w_r, u_s, u_r, a1_s, a1_r, a2_s, a2_r,
-    local_sem, fwd_ss, fwd_rs, out_ss, out_rs, back_ss, back_rs, ag_ss, ag_rs,
+    cb_acc, pb_acc, vec_acc,
+    w_s, w_r, u_s, u_r, a1_s, a1_r, a2_f, a2_s, a2_r,
+    local_sem, fwd_ss, fwd_rs, out_ss, out_rs, back_ss, back_rs,
+    agx_ss, agx_rs, agz_ss, agz_rs, agc_ss, agc_rs,
     emb_ss, emb_rs, w_ss, w_rs, u_ss, u_rs, a1_ss, a1_rs, a2_ss, a2_rs,
 ):
     T, D, SB, OC = dims["T"], dims["D"], dims["SB"], dims["OC"]
@@ -50,6 +51,10 @@
     d = lax.axis_index("dev")
     d_hi = lax.div(d, DY)
     d_y = lax.rem(d, DY)
+    t_zx = lax.div(t, 2)
+    t_core = lax.rem(t, 2)
+    t_z = lax.div(t, 4)
+    t_zx_beside = 2 * t_z + 1 - lax.rem(t_zx, 2)
 
     def dev(k):
         hi = lax.rem(d_hi + lax.div(k, DY), HI)
@@ -105,14 +110,33 @@
         return remote(
             back_s.at[c, j], back_r.at[c, who], back_ss.at[c, k], back_rs.at[c, who], (j, d))
 
-    def gather(c, k, who):
-        j = tow(k)
-        return remote(ag.at[c, t], ag.at[c, who], ag_ss.at[c, k], ag_rs.at[c, who], (j, d))
+    def pair(c, z, core):
+        return ag.at[c, pl.ds(2 * z, 2), core]
+
+    def gather_x(c, own):
+        zx = t_zx if own else t_zx_beside
+        src = ag.at[c, t_zx, t_core]
+        return remote(
+            src, ag.at[c, zx, t_core], agx_ss.at[c], agx_rs.at[c],
+            (2 * t_zx_beside + t_core, d))
+
+    def gather_z(c, k, own):
+        z = lax.rem(t_z + k, T // 4)
+        who = t_z if own else z
+        return remote(
+            pair(c, t_z, t_core), pair(c, who, t_core), agz_ss.at[c, k], agz_rs.at[c, who],
+            (4 * z + lax.rem(t, 4), d))
+
+    def gather_core(c, own):
+        core = t_core if own else 1 - t_core
+        return remote(
+            ag.at[c, :, t_core], ag.at[c, :, core], agc_ss.at[c], agc_rs.at[c],
+            (2 * t_zx + 1 - t_core, d))
 
     def emb_back(c, k, who):
         j = dev(k)
         return remote(
-            eg.at[c, j], emb_out.at[:, who, pl.ds(c * SC, SC), :],
+            eg.at[c, j], emb_land.at[:, who, pl.ds(c * SC, SC), :],
             emb_ss.at[c, k], emb_rs.at[c, who], (t, j))
 
     def over_dev(s, r, ss, rs):
@@ -135,7 +159,7 @@
 
     def emb_own(c):
         return pltpu.make_async_copy(
-            eg.at[c, d], emb_out.at[:, d, pl.ds(c * SC, SC), :], local_sem.at[NC + c])
+            eg.at[c, d], emb_land.at[:, d, pl.ds(c * SC, SC), :], local_sem.at[NC + c])
 
     weights = [
         pltpu.make_async_copy(src, dst, local_sem.at[2 * NC + i])
@@ -146,43 +170,46 @@
     def start_fwd(c):
         loop(1, D, lambda k: fwd(c, k).start())
 
-    for c in range(NC):
+    for c in range(2):
         start_fwd(c)
     for w in weights:
         w.start()
     for c in range(NC):
         fwd_own(c).start()
 
-    vw_acc[...] = jnp.zeros_like(vw_acc)
-    uw_acc[...] = jnp.zeros_like(uw_acc)
-    pw_acc[...] = jnp.zeros_like(pw_acc)
     cb_acc[...] = jnp.zeros_like(cb_acc)
     pb_acc[...] = jnp.zeros_like(pb_acc)
     vec_acc[...] = jnp.zeros_like(vec_acc)
     for w in weights:
         w.wait()
 
-    def chunk(c):
+    def forward(c):
+        slot = lax.rem(c, 3)
         fwd_own(c).wait()
         loop(1, D, lambda k: fwd_arrival(c, k).wait_recv())
-        low[...] = dot(base[c].reshape(R, W), tv[...]).astype(BF16)
+        low[c] = dot(base[c].reshape(R, W), tv[...]).astype(BF16)
 
         def forward_cols(j):
             at = cols(j, OC)
-            s = dot(low[...], tu[:, at]) + (cb[:, at] + 1.0)
-            scale[:, at] = s
+            s = dot(low[c], tu[:, at]) + (cb[:, at] + 1.0)
+            scale[slot, :, at] = s
             b = base[c, :, :, at].reshape(R, OC).astype(F32)
-            mixed[:, at] = (b * s).astype(BF16)
+            mixed[c, :, at] = (b * s).astype(BF16)
 
         loop(0, D, forward_cols)
-        pre = dot(mixed[...], pw[...]) + pb[...]
+        pre = dot(mixed[c], pw[...]) + pb[...]
         sig = jax.nn.sigmoid(pre)
-        sgrad[...] = sig * (1.0 + pre * (1.0 - sig))
+        sgrad[slot] = sig * (1.0 + pre * (1.0 - sig))
         out[c] = (pre * sig).astype(BF16).reshape(T, SC, PROJ)
         loop(1, T, lambda k: tower_out(c, k).start())
         arch_in[c, :, cols(t, PROJ)] = out[c, t]
+
+        @pl.when(c + 2 < NC)
+        def _():
+            start_fwd(c + 2)
+
+    def over_arch(c):
         loop(1, T, lambda k: tower_out_arrival(c, k).wait_recv())
-
         a_in = arch_in[c]
         a_low = dot(a_in, av[...]).astype(BF16)
         a_scale = dot(a_low, au[...]) + (ab[...] + 1.0)
@@ -195,41 +222,47 @@
             jnp.where(row == lane, jnp.broadcast_to(labels[...], (SC, SB)), 0.0),
             axis=1, keepdims=True)
         g = (jax.nn.sigmoid(logits) - label) * (LOSS_SCALE / (T * D * SB))
-        vec_acc[1:2, :] += jnp.sum(g * mix, axis=0, keepdims=True)
         g_mix = g * lw[...]
         g_cross = g_mix * a_f
-        vec_acc[0:1, :] += jnp.sum(g_cross, axis=0, keepdims=True)
-        g_cross_b = g_cross.astype(BF16)
-        g_low = dot_t(g_cross_b, au[...]).astype(BF16)
+        g_low = dot_t(g_cross.astype(BF16), au[...]).astype(BF16)
         g_in = (g_mix * a_scale + dot_t(g_low, av[...])).astype(BF16)
         for j in range(T):
-            back_s[c, j, :, 0:PROJ] = g_in[:, j * PROJ:(j + 1) * PROJ]
-            back_s[c, j, :, PROJ:2 * PROJ] = g_cross_b[:, j * PROJ:(j + 1) * PROJ]
+            back_s[c, j] = g_in[:, j * PROJ:(j + 1) * PROJ]
         loop(1, T, lambda k: back(c, k, t).start())
         back_r[c, t] = back_s[c, t]
-        ag[c, t, :, 0:AR] = a_low
-        ag[c, t, :, AR:2 * AR] = g_low
-        loop(1, T, lambda k: gather(c, k, t).start())
-
+        ag[c, t_zx, t_core, :, 0:AR] = a_low
+        ag[c, t_zx, t_core, :, AR:2 * AR] = g_low
+        g_wide = jnp.broadcast_to(g, (SC, PROJ))
+        g_high = g_wide.astype(BF16)
+        ag[c, t_zx, t_core, :, 2 * AR:2 * AR + PROJ] = g_high
+        ag[c, t_zx, t_core, :, 2 * AR + PROJ:] = (g_wide - g_high.astype(F32)).astype(BF16)
+        gather_x(c, True).start()
+        vec_acc[0:1, :] += jnp.sum(g_cross, axis=0, keepdims=True)
+        vec_acc[1:2, :] += jnp.sum(g * mix, axis=0, keepdims=True)
+
+    def backward(c):
+        slot = lax.rem(c, 3)
         loop(1, T, lambda k: back(c, k, tow(k)).wait_recv())
-        g_pre = back_r[c, :, :, 0:PROJ].reshape(R, PROJ).astype(F32) * sgrad[...]
+        gather_x(c, False).wait_recv()
+        loop(1, T // 4, lambda k: gather_z(c, k, True).start())
+        g_pre = back_r[c].reshape(R, PROJ).astype(F32) * sgrad[slot]
         pb_acc[...] += jnp.sum(g_pre, axis=0, keepdims=True)
-        gpre[...] = g_pre.astype(BF16)
+        gpre[c] = g_pre.astype(BF16)
 
         def backward_cols(j):
             at = cols(j, OC)
-            gm = dot_t(gpre[...], pw[at, :])
+            gm = dot_t(gpre[c], pw[at, :])
             gc = gm * base[c, :, :, at].reshape(R, OC).astype(F32)
             cb_acc[:, at] += jnp.sum(gc, axis=0, keepdims=True)
-            gcb[:, at] = gc.astype(BF16)
-            scale[:, at] = gm * scale[:, at]
+            gcb[c, :, at] = gc.astype(BF16)
+            scale[slot, :, at] = gm * scale[slot, :, at]
 
         loop(0, D, backward_cols)
-        glow[...] = dot_t(gcb[...], tu[...]).astype(BF16)
+        glow[c] = dot_t(gcb[c], tu[...]).astype(BF16)
 
         def grad_cols(j):
             at = cols(j, OC)
-            v = scale[:, at] + dot_t(glow[...], tv[at, :])
+            v = scale[slot, :, at] + dot_t(glow[c], tv[at, :])
             eg[c, j] = v.astype(BF16).reshape(T, SC, OC)
 
         def grad_send(k):
@@ -240,77 +273,91 @@
         grad_cols(d)
         emb_own(c).start()
 
-        glow_t = glow[...].T
-        low_t = low[...].T
-        gpre_t = gpre[...].T
-
-        def weight_cols(j):
-            at = cols(j, OC)
-            vw_acc[:, at] += dot(glow_t, base[c, :, :, at].reshape(R, OC))
-            uw_acc[:, at] += dot(low_t, gcb[:, at])
-            pw_acc[:, at] += dot(gpre_t, mixed[:, at])
-
-        loop(0, D, weight_cols)
-
-    loop(0, NC, chunk)
-
-    for c in range(NC):
-        loop(1, T, lambda k: gather(c, k, tow(k)).wait_recv())
-    gathered = ag[...].reshape(NC * R, 2 * AR)
-    gav = dot(out[...].reshape(NC * R, PROJ).T, gathered[:, AR:])
-    gau = dot(back_r[:, :, :, PROJ:].reshape(NC * R, PROJ).T, gathered[:, :AR]).T
+        @pl.when(c > 0)
+        def _():
+            gather_last(c - 1)
+
+    def gather_last(c):
+        loop(1, T // 4, lambda k: gather_z(c, k, False).wait_recv())
+        gather_core(c, True).start()
+
+    def step(i):
+        @pl.when(i < NC)
+        def _():
+            forward(i)
+
+        @pl.when(jnp.logical_and(i >= 1, i <= NC))
+        def _():
+            over_arch(i - 1)
+
+        @pl.when(i >= 2)
+        def _():
+            backward(i - 2)
+
+    loop(0, NC + 2, step)
+
+    N = NC * R
+    low_t = low[...].reshape(N, RANK).T
+
+    def u_cols(j):
+        at = cols(j, OC)
+        v = dot(low_t, gcb[:, :, at].reshape(N, OC))
+        u_s[:, :, at] = v.astype(BF16).reshape(D, RR, OC)
+
+    loop(0, D, u_cols)
+    loop(1, D, lambda k: u_copy(k, d).start())
+    u_r[d] = u_s[d]
+    gather_last(NC - 1)
+    glow_t = glow[...].reshape(N, RANK).T
+    gpre_t = gpre[...].reshape(N, PROJ).T
+    first = lax.broadcasted_iota(jnp.int32, (16, OC), 0) == 0
+    pb2 = jnp.broadcast_to(jnp.concatenate([pb_acc[...]] * (OC // PROJ), axis=1), (16, OC))
+
+    def w_cols(j):
+        at = cols(j, OC)
+        w_s[j, 0:RANK, :] = dot(glow_t, base[:, :, :, at].reshape(N, OC)).astype(BF16)
+        w_s[j, RANK:RANK + PROJ, :] = dot(gpre_t, mixed[:, :, at].reshape(N, OC)).astype(BF16)
+        w_s[j, RANK + PROJ:RANK + PROJ + 16, :] = jnp.where(
+            first, jnp.broadcast_to(cb_acc[:, at], (16, OC)), pb2).astype(BF16)
+
+    loop(0, D, w_cols)
+
+    loop(0, NC, lambda c: gather_core(c, False).wait_recv())
+    outs = out[...].reshape(N, PROJ)
+    factors = ag[...].reshape(N, 2 * AR + 2 * PROJ)
+    g = factors[:, 2 * AR:2 * AR + PROJ].astype(F32) + factors[:, 2 * AR + PROJ:].astype(F32)
+    g_cross_t = (g * lw[:, cols(t, PROJ)] * outs.astype(F32)).astype(BF16).T
+    gau = dot(g_cross_t, factors[:, :AR]).T
+    zeros = jnp.zeros((8, PROJ), F32)
     for j in range(T):
-        a1_s[j, 0:UR, :] = gau[j * UR:(j + 1) * UR, :]
-        a1_s[j, UR:UR + 8, :] = vec_acc[:, j * PROJ:(j + 1) * PROJ]
+        a1_s[j, 0:UR, :] = gau[j * UR:(j + 1) * UR, :].astype(BF16)
+        a1_s[j, UR:UR + 16, :] = jnp.concatenate(
+            [vec_acc[:, j * PROJ:(j + 1) * PROJ], zeros], axis=0).astype(BF16)
     loop(1, T, lambda k: a1_copy(k, t).start())
     a1_r[t] = a1_s[t]
+
+    loop(1, D, lambda k: w_copy(k, d).start())
+    w_r[d] = w_s[d]
+
+    gav = dot(outs.T, factors[:, AR:2 * AR])
     half = ARCH // 2
     for j in range(D):
-        a2_s[j, 8:16, 0:AR] = gav[j * AP:j * AP + 8, :]
-        a2_s[j, 8:16, AR:2 * AR] = gav[j * AP + 8:j * AP + 16, :]
-
+        a2_f[j, 8:16, 0:AR] = gav[j * AP:j * AP + 8, :]
+        a2_f[j, 8:16, AR:2 * AR] = gav[j * AP + 8:j * AP + 16, :]
+    loop(1, T, lambda k: a1_copy(k, tow(k)).wait_recv())
+    vec = jnp.sum(a1_r[:, UR:UR + 16, :].astype(F32), axis=0)
+    per = half // PROJ
+    for i in range(T):
+        part = a1_r[i, 0:UR, :].astype(F32)
+        r0 = UF * (i // per)
+        c0 = (i % per) * PROJ
+        for j in range(D):
+            a2_f[j, r0:r0 + UF, c0:c0 + PROJ] = part[j * UF:(j + 1) * UF, :]
     for j in range(D):
-        at = slice(j * OC, (j + 1) * OC)
-        u_s[j] = uw_acc[j * RR:(j + 1) * RR, :].astype(BF16)
-        w_s[j, 0:RANK, :] = vw_acc[:, at].astype(BF16)
-        w_s[j, RANK:RANK + PROJ, :] = pw_acc[:, at].astype(BF16)
-        first = lax.broadcasted_iota(jnp.int32, (16, OC), 0) == 0
-        pb2 = jnp.concatenate([pb_acc[...]] * (OC // PROJ), axis=1)
-        w_s[j, RANK + PROJ:RANK + PROJ + 16, :] = jnp.where(
-            first, jnp.broadcast_to(cb_acc[:, at], (16, OC)), jnp.broadcast_to(pb2, (16, OC))
-        ).astype(BF16)
-
-    def send_weights(k):
-        u_copy(k, d).start()
-        w_copy(k, d).start()
-
-    loop(1, D, send_weights)
-    u_r[d] = u_s[d]
-    w_r[d] = w_s[d]
-
-    loop(1, T, lambda k: a1_copy(k, tow(k)).wait_recv())
-    vec = jnp.sum(a1_r[:, UR:UR + 8, :], axis=0)
-    per = half // PROJ
-    for j in range(D):
-        for i in range(T):
-            r0 = UF * (i // per)
-            c0 = (i % per) * PROJ
-            a2_s[j, r0:r0 + UF, c0:c0 + PROJ] = a1_r[i, j * UF:(j + 1) * UF, :]
-        a2_s[j, 0:8, half:half + PROJ] = vec
-        a2_s[j, 8:16, half:half + PROJ] = vec
+        a2_f[j, :, half:half + PROJ] = vec
+    a2_s[...] = a2_f[...].astype(BF16)
     loop(1, D, lambda k: a2_copy(k, d).start())
     a2_r[d] = a2_s[d]
-
-    loop(1, D, lambda k: a2_copy(k, dev(k)).wait_recv())
-    a2 = jnp.sum(a2_r[...], axis=0)
-    gau_out[:, 0:half] = a2[0:UF, 0:half]
-    gau_out[:, half:] = a2[UF:2 * UF, 0:half]
-    gav_out[0:8, :] = a2[8:16, 0:AR]
-    gav_out[8:16, :] = a2[8:16, AR:2 * AR]
-    shift = lax.rem(PROJ - d * AP, PROJ)
-    vec = pltpu.roll(a2[0:8, half:half + PROJ], shift, 1)
-    gab_out[...] = vec[0:1, 0:AP]
-    glw_out[...] = vec[1:2, 0:AP]
 
     loop(1, D, lambda k: u_copy(k, dev(k)).wait_recv())
     loop(1, D, lambda k: w_copy(k, dev(k)).wait_recv())
@@ -319,8 +366,19 @@
     vw_out[...] = ws[0:RANK].T
     pw_out[...] = ws[RANK:RANK + PROJ].T
     cb_out[...] = ws[RANK + PROJ:RANK + PROJ + 1]
+    shift = lax.rem(PROJ - d * AP, PROJ)
     vec = pltpu.roll(ws[RANK + PROJ + 8:RANK + PROJ + 16, 0:PROJ], shift, 1)
     pb_out[...] = vec[0:1, 0:AP]
+
+    loop(1, D, lambda k: a2_copy(k, dev(k)).wait_recv())
+    a2 = jnp.sum(a2_r[...].astype(F32), axis=0)
+    gau_out[:, 0:half] = a2[0:UF, 0:half]
+    gau_out[:, half:] = a2[UF:2 * UF, 0:half]
+    gav_out[0:8, :] = a2[8:16, 0:AR]
+    gav_out[8:16, :] = a2[8:16, AR:2 * AR]
+    vec = pltpu.roll(a2[0:8, half:half + PROJ], shift, 1)
+    gab_out[...] = vec[0:1, 0:AP]
+    glw_out[...] = vec[1:2, 0:AP]
 
     for c in range(NC):
         emb_own(c).wait()
@@ -333,8 +391,10 @@
         def drain_tower(k):
             tower_out(c, k).wait_send()
             back(c, k, t).wait_send()
-            gather(c, k, t).wait_send()
-
+
+        gather_x(c, True).wait_send()
+        gather_core(c, True).wait_send()
+        loop(1, T // 4, lambda k: gather_z(c, k, True).wait_send())
         loop(1, D, drain_dev)
         loop(1, T, drain_tower)
 
@@ -345,6 +405,20 @@
 
     loop(1, D, drain_last)
     loop(1, T, lambda k: a1_copy(k, t).wait_send())
+
+
+def deliver(*refs):
+    n = (len(refs) - 1) // 2
+    src, dst, sem = refs[:n], refs[n:-1], refs[-1]
+    copies = [
+        pltpu.make_async_copy(src[0].at[i], dst[0].at[i], sem.at[i]) for i in range(src[0].shape[0])
+    ]
+    for copy in copies:
+        copy.start()
+    for a, b in zip(src[1:], dst[1:]):
+        b[...] = a[...]
+    for copy in copies:
+        copy.wait()
 
 
 def local(
@@ -364,6 +438,7 @@
     UR = AR // T
     AP = PROJ // D
     WR = RANK + PROJ + 16
+    AGW = 2 * AR + 2 * PROJ
     A2 = ARCH // 2 + PROJ
     dims = dict(T=T, D=D, SB=SB, OC=OC, RANK=RANK, PROJ=PROJ, AR=AR)
     vmem = pl.BlockSpec(memory_space=pltpu.VMEM)
@@ -392,22 +467,19 @@
             pltpu.VMEM((W, PROJ), BF16),
             pltpu.VMEM((ARCH, AR), BF16),
             pltpu.VMEM((AR, ARCH), BF16),
-            pltpu.VMEM((R, RANK), BF16),
-            pltpu.VMEM((R, W), F32),
-            pltpu.VMEM((R, W), BF16),
-            pltpu.VMEM((R, PROJ), F32),
-            pltpu.VMEM((R, PROJ), BF16),
-            pltpu.VMEM((R, W), BF16),
-            pltpu.VMEM((R, RANK), BF16),
+            pltpu.VMEM((NC, R, RANK), BF16),
+            pltpu.VMEM((3, R, W), F32),
+            pltpu.VMEM((NC, R, W), BF16),
+            pltpu.VMEM((3, R, PROJ), F32),
+            pltpu.VMEM((NC, R, PROJ), BF16),
+            pltpu.VMEM((NC, R, W), BF16),
+            pltpu.VMEM((NC, R, RANK), BF16),
             pltpu.VMEM((NC, T, SC, PROJ), BF16),
             pltpu.VMEM((NC, SC, ARCH), BF16),
-            pltpu.VMEM((NC, T, SC, 2 * PROJ), BF16),
-            pltpu.VMEM((NC, T, SC, 2 * PROJ), BF16),
-            pltpu.VMEM((NC, T, SC, 2 * AR), BF16),
+            pltpu.VMEM((NC, T, SC, PROJ), BF16),
+            pltpu.VMEM((NC, T, SC, PROJ), BF16),
+            pltpu.VMEM((NC, T // 2, 2, SC, AGW), BF16),
             pltpu.VMEM((NC, D, T, SC, OC), BF16),
-            pltpu.VMEM((RANK, W), F32),
-            pltpu.VMEM((RANK, W), F32),
-            pltpu.VMEM((PROJ, W), F32),
             pltpu.VMEM((1, W), F32),
             pltpu.VMEM((1, PROJ), F32),
             pltpu.VMEM((8, ARCH), F32),
@@ -415,15 +487,18 @@
             pltpu.VMEM((D, WR, OC), BF16),
             pltpu.VMEM((D, RANK // D, W), BF16),
             pltpu.VMEM((D, RANK // D, W), BF16),
-            pltpu.VMEM((T, UR + 8, PROJ), F32),
-            pltpu.VMEM((T, UR + 8, PROJ), F32),
+            pltpu.VMEM((T, UR + 16, PROJ), BF16),
+            pltpu.VMEM((T, UR + 16, PROJ), BF16),
             pltpu.VMEM((D, 16, A2), F32),
-            pltpu.VMEM((D, 16, A2), F32),
+            pltpu.VMEM((D, 16, A2), BF16),
+            pltpu.VMEM((D, 16, A2), BF16),
             dma((2 * NC + 5,)),
             dma((NC, D)), dma((NC, D)),
             dma((NC, T)), dma((NC, T)),
             dma((NC, T)), dma((NC, T)),
-            dma((NC, T)), dma((NC, T)),
+            dma((NC,)), dma((NC,)),
+            dma((NC, T // 4)), dma((NC, T // 4)),
+            dma((NC,)), dma((NC,)),
             dma((NC, D)), dma((NC, D)),
             dma((D,)), dma((D,)),
             dma((D,)), dma((D,)),
@@ -437,7 +512,14 @@
         embeddings.reshape(T, D, SB, OC), tower_v[0], tower_u[0], cross_bias, proj_w[0], proj_bias,
         arch_v, arch_u, arch_bias[None], logit_w[None], labels[None],
     )
-    eg, vw, uw, cb, pw, pb, gav, gau, gab, glw = outs
+    eg, vw, uw, cb, pw, pb, gav, gau, gab, glw = pl.pallas_call(
+        deliver,
+        out_shape=tuple(jax.ShapeDtypeStruct(x.shape, x.dtype) for x in outs),
+        in_specs=[hbm] + [vmem] * 9,
+        out_specs=(hbm,) + (vmem,) * 9,
+        scratch_shapes=[dma((T,))],
+        compiler_params=pltpu.CompilerParams(vmem_limit_bytes=8 << 20),
+    )(*outs)
     return (
         eg.reshape(rows, OC), vw[None], uw[None], cb, pw[None], pb,
         gav, gau, gab[0], glw[0],

time: 202 us -> 177 us (0.88)
  Pallas kernels: 191 us -> 166 us
    pallas_call x1, Pallas kernels: 191 us -> 163 us  [local(): pl.pallas_call(functools.partial(kernel, dims), out_shape=(jax.ShapeDtype...]
    pallas_call x0 -> x1, Pallas kernels: none -> 2.99 us  [local(): pl.pallas_call(deliver, out_shape=tuple((jax.ShapeDtypeStruct(x.shape, x....]
    unnamed x28 -> x20, local copies, waits for them, and re-layouts: 9.94 us -> 9.09 us
where the time goes in v2:
time: 177 us; the launch traced here: 176 us
  Pallas kernels  166 us (94%)
  local copies, waits for them, and re-layouts  9.09 us (5%)
    pallas_call x1, Pallas kernels, local(): pl.pallas_call(functools.partial(kernel, dims), out_shape=(jax.ShapeDtype...  163 us
    unnamed x20, local copies, waits for them, and re-layouts  9.09 us

profile of v2, /device:TPU:1, one launch (start us, length us, event | category | flops | bytes accessed | tf_op | source)
XLA Modules:
  0.0 176.2 jit_solution(7912848541865165024)
XLA Ops:
  0.6 163.4 %shard_map.186 = (bf16[16,8,64,256]{3,2,1,0:T(8,128)(2,1)}, f32[256,256]{1,0:T(8,128)}, f32[32,2048]{1,0:T(8,128)}, f32[1,256]{1,0:T(1,128)}, f32[256,128]{1,0:T...) custom-call(bf16[16,8,64,256]{3,2,1,0:T(8,128)(2,1)} %bitcast.13, ...), custom_call_target="tpu_custom_call" | custom-call | tf_op jit(solution)/shard_map/pallas_call | solution.py:447
  164.1 0.0 copy-start
  164.1 2.2 %copy-done = bf16[16,8,64,256]{3,2,1,0:T(8,128)(2,1)S(1)} copy-done((bf16[16,8,64,256]{3,2,1,0:T(8,128)(2,1)S(1)}, bf16[16,8,64,256]{3,2,1,0:T(8,128)(2,1)}, u32[]{:S(2)}) %copy-start) | copy-done | bytes 4194328
  166.3 0.0 copy-start.1
  166.3 0.9 copy-done.1
  167.2 0.0 copy-start.2
  167.2 0.9 copy-done.2
  168.2 0.0 copy-start.3
  168.2 0.9 copy-done.3
  169.1 0.0 copy-start.4
  169.1 0.8 copy-done.4
  169.8 0.0 copy-start.5
  169.8 0.8 copy-done.5
  170.6 0.0 copy-start.6
  170.6 0.6 copy-done.6
  171.2 0.0 copy-start.7
  171.2 0.7 copy-done.7
  171.9 0.0 copy-start.8
  171.9 0.7 copy-done.8
  172.6 0.0 copy-start.9
  172.6 0.6 copy-done.9
  173.2 3.0 %shard_map.187 = (bf16[16,8,64,256]{3,2,1,0:T(8,128)(2,1)}, f32[256,256]{1,0:T(8,128)}, f32[32,2048]{1,0:T(8,128)}, f32[1,256]{1,0:T(1,128)}, f32[256,128]{1,0:T...) custom-call(bf16[16,8,64,256]{3,2,1,0:T(8,128)(2,1)S(1)} %copy-done,, ...), custom_call_target="tpu_custom_call" | custom-call | tf_op jit(solution)/shard_map/pallas_call | solution.py:515
Async XLA Ops:
  164.1 2.2 %copy-start = (bf16[16,8,64,256]{3,2,1,0:T(8,128)(2,1)S(1)}, bf16[16,8,64,256]{3,2,1,0:T(8,128)(2,1)}, u32[]{:S(2)}) copy-start(bf16[16,8,64,256]{3,2,1,0:T(8,128)(2,1)} %get-tuple-element.30.refs_0_) | copy-start | bytes 12582916
  166.3 0.9 copy-start.1
  167.2 0.9 copy-start.2
  168.2 0.9 copy-start.3
  169.1 0.8 copy-start.4
  169.8 0.8 copy-start.5
  170.6 0.6 copy-start.6
  171.2 0.7 copy-start.7
  171.9 0.7 copy-start.8
  172.6 0.6 copy-start.9

commit v3 on v2

--- a/solution.py
+++ b/solution.py
@@ -30,10 +30,10 @@
     low, scale, mixed, sgrad, gpre, gcb, glow,
     out, arch_in, back_s, back_r, ag, eg,
     cb_acc, pb_acc, vec_acc,
-    w_s, w_r, u_s, u_r, a1_s, a1_r, a2_f, a2_s, a2_r,
+    w_s, w_r, w_xs, w_xr, u_s, u_t, u_r, u_xr, a1_s, a1_r, a2_f, a2_s, a2_r,
     local_sem, fwd_ss, fwd_rs, out_ss, out_rs, back_ss, back_rs,
     agx_ss, agx_rs, agz_ss, agz_rs, agc_ss, agc_rs,
-    emb_ss, emb_rs, w_ss, w_rs, u_ss, u_rs, a1_ss, a1_rs, a2_ss, a2_rs,
+    emb_ss, emb_rs, w_ss, w_rs, wx_ss, wx_rs, u_ss, u_rs, ux_ss, ux_rs, a1_ss, a1_rs, a2_ss, a2_rs,
 ):
     T, D, SB, OC = dims["T"], dims["D"], dims["SB"], dims["OC"]
     HI = 2
@@ -57,6 +57,7 @@
     t_zx_beside = 2 * t_z + 1 - lax.rem(t_zx, 2)
 
     def dev(k):
+        k = lax.rem(k, 2) * DY + lax.div(k, 2)
         hi = lax.rem(d_hi + lax.div(k, DY), HI)
         return hi * DY + lax.rem(d_y + lax.rem(k, DY), DY)
 
@@ -64,10 +65,16 @@
         return lax.rem(t + k, T)
 
     def cols(j, n):
+        if isinstance(j, int):
+            return slice(j * n, (j + 1) * n)
         return pl.ds(pl.multiple_of(j * n, n), n)
 
     def loop(lo, hi, f):
         lax.fori_loop(lo, hi, lambda i, x: (f(i), x)[1], 0)
+
+    def unrolled(lo, hi, f):
+        for i in range(lo, hi):
+            f(i)
 
     def remote(src, dst, ss, rs, who):
         return pltpu.make_async_remote_copy(
@@ -145,8 +152,37 @@
             return remote(s.at[j], r.at[who], ss.at[k], rs.at[who], (t, j))
         return make
 
-    w_copy = over_dev(w_s, w_r, w_ss, w_rs)
-    u_copy = over_dev(u_s, u_r, u_ss, u_rs)
+    def along_y(s, r, ss, rs):
+        def make(k, own):
+            y = lax.rem(d_y + k, DY)
+            who = d_y if own else y
+            return remote(
+                s.at[:, y], r.at[who], ss.at[k], rs.at[who], (t, d_hi * DY + y))
+        return make
+
+    def across_x(s, r, ss, rs):
+        return remote(s, r, ss.at[0], rs.at[0], (t, (1 - d_hi) * DY + d_y))
+
+    w_copy = along_y(w_s, w_r, w_ss, w_rs)
+
+    def u_copy(k, own):
+        y = lax.rem(d_y + k, DY)
+        who = d_y if own else y
+        return remote(
+            u_t.at[y], u_r.at[who], u_ss.at[k], u_rs.at[who], (t, d_hi * DY + y))
+
+    def w_across():
+        return across_x(w_xs, w_xr, wx_ss, wx_rs)
+
+    def u_across():
+        return across_x(u_s.at[1 - d_hi], u_xr, ux_ss, ux_rs)
+
+    def partial(r, hi):
+        total = r[0, hi].astype(F32)
+        for y in range(1, DY):
+            total += r[y, hi].astype(F32)
+        return total
+
     a2_copy = over_dev(a2_s, a2_r, a2_ss, a2_rs)
 
     def a1_copy(k, who):
@@ -196,7 +232,7 @@
             b = base[c, :, :, at].reshape(R, OC).astype(F32)
             mixed[c, :, at] = (b * s).astype(BF16)
 
-        loop(0, D, forward_cols)
+        unrolled(0, D, forward_cols)
         pre = dot(mixed[c], pw[...]) + pb[...]
         sig = jax.nn.sigmoid(pre)
         sgrad[slot] = sig * (1.0 + pre * (1.0 - sig))
@@ -257,7 +293,7 @@
             gcb[c, :, at] = gc.astype(BF16)
             scale[slot, :, at] = gm * scale[slot, :, at]
 
-        loop(0, D, backward_cols)
+        unrolled(0, D, backward_cols)
         glow[c] = dot_t(gcb[c], tu[...]).astype(BF16)
 
         def grad_cols(j):
@@ -266,10 +302,10 @@
             eg[c, j] = v.astype(BF16).reshape(T, SC, OC)
 
         def grad_send(k):
-            grad_cols(dev(k))
-            emb_back(c, k, d).start()
-
-        loop(1, D, grad_send)
+            grad_cols(dev(jnp.int32(k)))
+            emb_back(c, jnp.int32(k), d).start()
+
+        unrolled(1, D, grad_send)
         grad_cols(d)
         emb_own(c).start()
 
@@ -296,18 +332,17 @@
 
     loop(0, NC + 2, step)
 
+    gather_last(NC - 1)
     N = NC * R
     low_t = low[...].reshape(N, RANK).T
 
     def u_cols(j):
         at = cols(j, OC)
         v = dot(low_t, gcb[:, :, at].reshape(N, OC))
-        u_s[:, :, at] = v.astype(BF16).reshape(D, RR, OC)
-
-    loop(0, D, u_cols)
-    loop(1, D, lambda k: u_copy(k, d).start())
-    u_r[d] = u_s[d]
-    gather_last(NC - 1)
+        u_s[:, :, :, at] = v.astype(BF16).reshape(HI, DY, RR, OC)
+
+    unrolled(0, D, u_cols)
+    u_across().start()
     glow_t = glow[...].reshape(N, RANK).T
     gpre_t = gpre[...].reshape(N, PROJ).T
     first = lax.broadcasted_iota(jnp.int32, (16, OC), 0) == 0
@@ -315,12 +350,15 @@
 
     def w_cols(j):
         at = cols(j, OC)
-        w_s[j, 0:RANK, :] = dot(glow_t, base[:, :, :, at].reshape(N, OC)).astype(BF16)
-        w_s[j, RANK:RANK + PROJ, :] = dot(gpre_t, mixed[:, :, at].reshape(N, OC)).astype(BF16)
-        w_s[j, RANK + PROJ:RANK + PROJ + 16, :] = jnp.where(
+        hi, y = j // DY, j % DY
+        w_s[hi, y, 0:RANK, :] = dot(glow_t, base[:, :, :, at].reshape(N, OC)).astype(BF16)
+        w_s[hi, y, RANK:RANK + PROJ, :] = dot(gpre_t, mixed[:, :, at].reshape(N, OC)).astype(BF16)
+        w_s[hi, y, RANK + PROJ:RANK + PROJ + 16, :] = jnp.where(
             first, jnp.broadcast_to(cb_acc[:, at], (16, OC)), pb2).astype(BF16)
 
-    loop(0, D, w_cols)
+    unrolled(0, D, w_cols)
+    loop(1, DY, lambda k: w_copy(k, True).start())
+    w_r[d_y] = w_s[:, d_y]
 
     loop(0, NC, lambda c: gather_core(c, False).wait_recv())
     outs = out[...].reshape(N, PROJ)
@@ -336,8 +374,11 @@
     loop(1, T, lambda k: a1_copy(k, t).start())
     a1_r[t] = a1_s[t]
 
-    loop(1, D, lambda k: w_copy(k, d).start())
-    w_r[d] = w_s[d]
+
+    u_across().wait_recv()
+    u_t[...] = (u_s[d_hi].astype(F32) + u_xr[...].astype(F32)).astype(BF16)
+    loop(1, DY, lambda k: u_copy(k, True).start())
+    u_r[d_y] = u_t[d_y]
 
     gav = dot(outs.T, factors[:, AR:2 * AR])
     half = ARCH // 2
@@ -359,10 +400,14 @@
     loop(1, D, lambda k: a2_copy(k, d).start())
     a2_r[d] = a2_s[d]
 
-    loop(1, D, lambda k: u_copy(k, dev(k)).wait_recv())
-    loop(1, D, lambda k: w_copy(k, dev(k)).wait_recv())
+    loop(1, DY, lambda k: w_copy(k, False).wait_recv())
+    w_xs[...] = partial(w_r, 1 - d_hi).astype(BF16)
+    w_across().start()
+    loop(1, DY, lambda k: u_copy(k, False).wait_recv())
     uw_out[...] = jnp.sum(u_r[...].astype(F32), axis=0)
-    ws = jnp.sum(w_r[...].astype(F32), axis=0)
+    w_own = partial(w_r, d_hi)
+    w_across().wait_recv()
+    ws = w_own + w_xr[...].astype(F32)
     vw_out[...] = ws[0:RANK].T
     pw_out[...] = ws[RANK:RANK + PROJ].T
     cb_out[...] = ws[RANK + PROJ:RANK + PROJ + 1]
@@ -399,25 +444,41 @@
         loop(1, T, drain_tower)
 
     def drain_last(k):
-        u_copy(k, d).wait_send()
-        w_copy(k, d).wait_send()
         a2_copy(k, d).wait_send()
 
     loop(1, D, drain_last)
+
+    def drain_weights(k):
+        u_copy(k, True).wait_send()
+        w_copy(k, True).wait_send()
+
+    loop(1, DY, drain_weights)
+    u_across().wait_send()
+    w_across().wait_send()
     loop(1, T, lambda k: a1_copy(k, t).wait_send())
 
 
-def deliver(*refs):
-    n = (len(refs) - 1) // 2
-    src, dst, sem = refs[:n], refs[n:-1], refs[-1]
-    copies = [
-        pltpu.make_async_copy(src[0].at[i], dst[0].at[i], sem.at[i]) for i in range(src[0].shape[0])
+def deliver(n, *refs):
+    src, dst, held, sem_in, sem_out = refs[:n], refs[n:2 * n], refs[2 * n:3 * n], refs[-2], refs[-1]
+    parts = [(0, i) for i in range(src[0].shape[0])] + [(a, None) for a in range(1, n)]
+
+    def at(ref, i):
+        return ref if i is None else ref.at[i]
+
+    into = [
+        pltpu.make_async_copy(at(src[a], i), at(held[a], i), sem_in.at[k])
+        for k, (a, i) in enumerate(parts)
     ]
-    for copy in copies:
+    away = [
+        pltpu.make_async_copy(at(held[a], i), at(dst[a], i), sem_out.at[k])
+        for k, (a, i) in enumerate(parts)
+    ]
+    for copy in into:
         copy.start()
-    for a, b in zip(src[1:], dst[1:]):
-        b[...] = a[...]
-    for copy in copies:
+    for copy, onward in zip(into, away):
+        copy.wait()
+        onward.start()
+    for copy in away:
         copy.wait()
 
 
@@ -483,10 +544,14 @@
             pltpu.VMEM((1, W), F32),
             pltpu.VMEM((1, PROJ), F32),
             pltpu.VMEM((8, ARCH), F32),
-            pltpu.VMEM((D, WR, OC), BF16),
-            pltpu.VMEM((D, WR, OC), BF16),
-            pltpu.VMEM((D, RANK // D, W), BF16),
-            pltpu.VMEM((D, RANK // D, W), BF16),
+            pltpu.VMEM((2, D // 2, WR, OC), BF16),
+            pltpu.VMEM((D // 2, 2, WR, OC), BF16),
+            pltpu.VMEM((WR, OC), BF16),
+            pltpu.VMEM((WR, OC), BF16),
+            pltpu.VMEM((2, D // 2, RANK // D, W), BF16),
+            pltpu.VMEM((D // 2, RANK // D, W), BF16),
+            pltpu.VMEM((D // 2, RANK // D, W), BF16),
+            pltpu.VMEM((D // 2, RANK // D, W), BF16),
             pltpu.VMEM((T, UR + 16, PROJ), BF16),
             pltpu.VMEM((T, UR + 16, PROJ), BF16),
             pltpu.VMEM((D, 16, A2), F32),
@@ -500,8 +565,8 @@
             dma((NC, T // 4)), dma((NC, T // 4)),
             dma((NC,)), dma((NC,)),
             dma((NC, D)), dma((NC, D)),
-            dma((D,)), dma((D,)),
-            dma((D,)), dma((D,)),
+            dma((D // 2,)), dma((D // 2,)), dma((1,)), dma((1,)),
+            dma((D // 2,)), dma((D // 2,)), dma((1,)), dma((1,)),
             dma((T,)), dma((T,)),
             dma((D,)), dma((D,)),
         ],
@@ -512,13 +577,15 @@
         embeddings.reshape(T, D, SB, OC), tower_v[0], tower_u[0], cross_bias, proj_w[0], proj_bias,
         arch_v, arch_u, arch_bias[None], logit_w[None], labels[None],
     )
+    n = len(outs)
     eg, vw, uw, cb, pw, pb, gav, gau, gab, glw = pl.pallas_call(
-        deliver,
+        functools.partial(deliver, n),
         out_shape=tuple(jax.ShapeDtypeStruct(x.shape, x.dtype) for x in outs),
-        in_specs=[hbm] + [vmem] * 9,
-        out_specs=(hbm,) + (vmem,) * 9,
-        scratch_shapes=[dma((T,))],
-        compiler_params=pltpu.CompilerParams(vmem_limit_bytes=8 << 20),
+        in_specs=[hbm] * n,
+        out_specs=(hbm,) * n,
+        scratch_shapes=[pltpu.VMEM(x.shape, x.dtype) for x in outs]
+        + [dma((T + n - 1,)), dma((T + n - 1,))],
+        compiler_params=pltpu.CompilerParams(vmem_limit_bytes=60 << 20),
     )(*outs)
     return (
         eg.reshape(rows, OC), vw[None], uw[None], cb, pw[None], pb,

time: 177 us -> 153 us (0.86)
  Pallas kernels: 166 us -> 152 us
  local copies, waits for them, and re-layouts: 9.09 us -> 0 us
    pallas_call x1, Pallas kernels: 163 us -> 148 us  [local(): pl.pallas_call(functools.partial(kernel, dims), out_shape=(jax.ShapeDtype...]
    unnamed x20 -> x0, local copies, waits for them, and re-layouts: 9.09 us -> none
where the time goes in v3:
time: 153 us
  Pallas kernels  152 us (99%)
    pallas_call x1, Pallas kernels, local(): pl.pallas_call(functools.partial(kernel, dims), out_shape=(jax.ShapeDtype...  148 us
    pallas_call x1, Pallas kernels, local(): pl.pallas_call(functools.partial(deliver, n), out_shape=tuple((jax.ShapeD...  4.68 us

profile of v3, /device:TPU:1, one launch (start us, length us, event | category | flops | bytes accessed | tf_op | source)
XLA Modules:
  0.0 152.9 jit_solution(547035272040799525)
XLA Ops:
  0.6 147.6 %shard_map.186 = (bf16[16,8,64,256]{3,2,1,0:T(8,128)(2,1)}, f32[256,256]{1,0:T(8,128)}, f32[32,2048]{1,0:T(8,128)}, f32[1,256]{1,0:T(1,128)}, f32[256,128]{1,0:T...) custom-call(bf16[16,8,64,256]{3,2,1,0:T(8,128)(2,1)} %bitcast.13, ...), custom_call_target="tpu_custom_call" | custom-call | tf_op jit(solution)/shard_map/pallas_call | solution.py:508
  148.3 4.7 %shard_map.187 = (bf16[16,8,64,256]{3,2,1,0:T(8,128)(2,1)}, f32[256,256]{1,0:T(8,128)}, f32[32,2048]{1,0:T(8,128)}, f32[1,256]{1,0:T(1,128)}, f32[256,128]{1,0:T...) custom-call(bf16[16,8,64,256]{3,2,1,0:T(8,128)(2,1)} %get-tuple-elem, ...), custom_call_target="tpu_custom_call" | custom-call | tf_op jit(solution)/shard_map/pallas_call | solution.py:581

commit v4 on v3

--- a/solution.py
+++ b/solution.py
@@ -30,10 +30,10 @@
     low, scale, mixed, sgrad, gpre, gcb, glow,
     out, arch_in, back_s, back_r, ag, eg,
     cb_acc, pb_acc, vec_acc,
-    w_s, w_r, w_xs, w_xr, u_s, u_t, u_r, u_xr, a1_s, a1_r, a2_f, a2_s, a2_r,
+    w_s, w_r, w_xs, w_xr, p_s, p_r, p_xs, p_xr, u_s, u_t, u_r, u_xr, a1_s, a1_r, a2_f, a2_s, a2_r,
     local_sem, fwd_ss, fwd_rs, out_ss, out_rs, back_ss, back_rs,
     agx_ss, agx_rs, agz_ss, agz_rs, agc_ss, agc_rs,
-    emb_ss, emb_rs, w_ss, w_rs, wx_ss, wx_rs, u_ss, u_rs, ux_ss, ux_rs, a1_ss, a1_rs, a2_ss, a2_rs,
+    emb_ss, emb_rs, w_ss, w_rs, wx_ss, wx_rs, p_ss, p_rs, px_ss, px_rs, u_ss, u_rs, ux_ss, ux_rs, a1_ss, a1_rs, a2_ss, a2_rs,
 ):
     T, D, SB, OC = dims["T"], dims["D"], dims["SB"], dims["OC"]
     HI = 2
@@ -164,12 +164,16 @@
         return remote(s, r, ss.at[0], rs.at[0], (t, (1 - d_hi) * DY + d_y))
 
     w_copy = along_y(w_s, w_r, w_ss, w_rs)
+    p_copy = along_y(p_s, p_r, p_ss, p_rs)
 
     def u_copy(k, own):
         y = lax.rem(d_y + k, DY)
         who = d_y if own else y
         return remote(
             u_t.at[y], u_r.at[who], u_ss.at[k], u_rs.at[who], (t, d_hi * DY + y))
+
+    def p_across():
+        return across_x(p_xs, p_xr, px_ss, px_rs)
 
     def w_across():
         return across_x(w_xs, w_xr, wx_ss, wx_rs)
@@ -220,7 +224,7 @@
         w.wait()
 
     def forward(c):
-        slot = lax.rem(c, 3)
+        slot = lax.rem(c, 4)
         fwd_own(c).wait()
         loop(1, D, lambda k: fwd_arrival(c, k).wait_recv())
         low[c] = dot(base[c].reshape(R, W), tv[...]).astype(BF16)
@@ -277,7 +281,7 @@
         vec_acc[1:2, :] += jnp.sum(g * mix, axis=0, keepdims=True)
 
     def backward(c):
-        slot = lax.rem(c, 3)
+        slot = lax.rem(c, 4)
         loop(1, T, lambda k: back(c, k, tow(k)).wait_recv())
         gather_x(c, False).wait_recv()
         loop(1, T // 4, lambda k: gather_z(c, k, True).start())
@@ -326,23 +330,14 @@
         def _():
             over_arch(i - 1)
 
-        @pl.when(i >= 2)
+        @pl.when(i >= 3)
         def _():
-            backward(i - 2)
-
-    loop(0, NC + 2, step)
+            backward(i - 3)
+
+    loop(0, NC + 3, step)
 
     gather_last(NC - 1)
     N = NC * R
-    low_t = low[...].reshape(N, RANK).T
-
-    def u_cols(j):
-        at = cols(j, OC)
-        v = dot(low_t, gcb[:, :, at].reshape(N, OC))
-        u_s[:, :, :, at] = v.astype(BF16).reshape(HI, DY, RR, OC)
-
-    unrolled(0, D, u_cols)
-    u_across().start()
     glow_t = glow[...].reshape(N, RANK).T
     gpre_t = gpre[...].reshape(N, PROJ).T
     first = lax.broadcasted_iota(jnp.int32, (16, OC), 0) == 0
@@ -351,14 +346,21 @@
     def w_cols(j):
         at = cols(j, OC)
         hi, y = j // DY, j % DY
-        w_s[hi, y, 0:RANK, :] = dot(glow_t, base[:, :, :, at].reshape(N, OC)).astype(BF16)
-        w_s[hi, y, RANK:RANK + PROJ, :] = dot(gpre_t, mixed[:, :, at].reshape(N, OC)).astype(BF16)
-        w_s[hi, y, RANK + PROJ:RANK + PROJ + 16, :] = jnp.where(
+        w_s[hi, y] = dot(glow_t, base[:, :, :, at].reshape(N, OC)).astype(BF16)
+
+    def p_cols(j):
+        at = cols(j, OC)
+        hi, y = j // DY, j % DY
+        p_s[hi, y, 0:PROJ, :] = dot(gpre_t, mixed[:, :, at].reshape(N, OC)).astype(BF16)
+        p_s[hi, y, PROJ:PROJ + 16, :] = jnp.where(
             first, jnp.broadcast_to(cb_acc[:, at], (16, OC)), pb2).astype(BF16)
 
     unrolled(0, D, w_cols)
     loop(1, DY, lambda k: w_copy(k, True).start())
     w_r[d_y] = w_s[:, d_y]
+    unrolled(0, D, p_cols)
+    loop(1, DY, lambda k: p_copy(k, True).start())
+    p_r[d_y] = p_s[:, d_y]
 
     loop(0, NC, lambda c: gather_core(c, False).wait_recv())
     outs = out[...].reshape(N, PROJ)
@@ -373,15 +375,19 @@
             [vec_acc[:, j * PROJ:(j + 1) * PROJ], zeros], axis=0).astype(BF16)
     loop(1, T, lambda k: a1_copy(k, t).start())
     a1_r[t] = a1_s[t]
-
-
-    u_across().wait_recv()
-    u_t[...] = (u_s[d_hi].astype(F32) + u_xr[...].astype(F32)).astype(BF16)
-    loop(1, DY, lambda k: u_copy(k, True).start())
-    u_r[d_y] = u_t[d_y]
-
+    low_t = low[...].reshape(N, RANK).T
+
+    def u_cols(j):
+        at = cols(j, OC)
+        v = dot(low_t, gcb[:, :, at].reshape(N, OC))
+        u_s[:, :, :, at] = v.astype(BF16).reshape(HI, DY, RR, OC)
+
+    unrolled(0, D, u_cols)
+    u_across().start()
+
+
+    half = ARCH // 2
     gav = dot(outs.T, factors[:, AR:2 * AR])
-    half = ARCH // 2
     for j in range(D):
         a2_f[j, 8:16, 0:AR] = gav[j * AP:j * AP + 8, :]
         a2_f[j, 8:16, AR:2 * AR] = gav[j * AP + 8:j * AP + 16, :]
@@ -399,20 +405,30 @@
     a2_s[...] = a2_f[...].astype(BF16)
     loop(1, D, lambda k: a2_copy(k, d).start())
     a2_r[d] = a2_s[d]
+    u_across().wait_recv()
+    u_t[...] = (u_s[d_hi].astype(F32) + u_xr[...].astype(F32)).astype(BF16)
+    loop(1, DY, lambda k: u_copy(k, True).start())
+    u_r[d_y] = u_t[d_y]
+
 
     loop(1, DY, lambda k: w_copy(k, False).wait_recv())
     w_xs[...] = partial(w_r, 1 - d_hi).astype(BF16)
     w_across().start()
+    loop(1, DY, lambda k: p_copy(k, False).wait_recv())
+    p_xs[...] = partial(p_r, 1 - d_hi).astype(BF16)
+    p_across().start()
     loop(1, DY, lambda k: u_copy(k, False).wait_recv())
     uw_out[...] = jnp.sum(u_r[...].astype(F32), axis=0)
     w_own = partial(w_r, d_hi)
     w_across().wait_recv()
-    ws = w_own + w_xr[...].astype(F32)
-    vw_out[...] = ws[0:RANK].T
-    pw_out[...] = ws[RANK:RANK + PROJ].T
-    cb_out[...] = ws[RANK + PROJ:RANK + PROJ + 1]
+    vw_out[...] = (w_own + w_xr[...].astype(F32)).T
+    p_own = partial(p_r, d_hi)
+    p_across().wait_recv()
+    ps = p_own + p_xr[...].astype(F32)
+    pw_out[...] = ps[0:PROJ].T
+    cb_out[...] = ps[PROJ:PROJ + 1]
     shift = lax.rem(PROJ - d * AP, PROJ)
-    vec = pltpu.roll(ws[RANK + PROJ + 8:RANK + PROJ + 16, 0:PROJ], shift, 1)
+    vec = pltpu.roll(ps[PROJ + 8:PROJ + 16, 0:PROJ], shift, 1)
     pb_out[...] = vec[0:1, 0:AP]
 
     loop(1, D, lambda k: a2_copy(k, dev(k)).wait_recv())
@@ -451,10 +467,12 @@
     def drain_weights(k):
         u_copy(k, True).wait_send()
         w_copy(k, True).wait_send()
+        p_copy(k, True).wait_send()
 
     loop(1, DY, drain_weights)
     u_across().wait_send()
     w_across().wait_send()
+    p_across().wait_send()
     loop(1, T, lambda k: a1_copy(k, t).wait_send())
 
 
@@ -498,7 +516,7 @@
     ARCH, AR = arch_v.shape
     UR = AR // T
     AP = PROJ // D
-    WR = RANK + PROJ + 16
+    PR = PROJ + 16
     AGW = 2 * AR + 2 * PROJ
     A2 = ARCH // 2 + PROJ
     dims = dict(T=T, D=D, SB=SB, OC=OC, RANK=RANK, PROJ=PROJ, AR=AR)
@@ -529,9 +547,9 @@
             pltpu.VMEM((ARCH, AR), BF16),
             pltpu.VMEM((AR, ARCH), BF16),
             pltpu.VMEM((NC, R, RANK), BF16),
-            pltpu.VMEM((3, R, W), F32),
+            pltpu.VMEM((4, R, W), F32),
             pltpu.VMEM((NC, R, W), BF16),
-            pltpu.VMEM((3, R, PROJ), F32),
+            pltpu.VMEM((4, R, PROJ), F32),
             pltpu.VMEM((NC, R, PROJ), BF16),
             pltpu.VMEM((NC, R, W), BF16),
             pltpu.VMEM((NC, R, RANK), BF16),
@@ -544,10 +562,14 @@
             pltpu.VMEM((1, W), F32),
             pltpu.VMEM((1, PROJ), F32),
             pltpu.VMEM((8, ARCH), F32),
-            pltpu.VMEM((2, D // 2, WR, OC), BF16),
-            pltpu.VMEM((D // 2, 2, WR, OC), BF16),
-            pltpu.VMEM((WR, OC), BF16),
-            pltpu.VMEM((WR, OC), BF16),
+            pltpu.VMEM((2, D // 2, RANK, OC), BF16),
+            pltpu.VMEM((D // 2, 2, RANK, OC), BF16),
+            pltpu.VMEM((RANK, OC), BF16),
+            pltpu.VMEM((RANK, OC), BF16),
+            pltpu.VMEM((2, D // 2, PR, OC), BF16),
+            pltpu.VMEM((D // 2, 2, PR, OC), BF16),
+            pltpu.VMEM((PR, OC), BF16),
+            pltpu.VMEM((PR, OC), BF16),
             pltpu.VMEM((2, D // 2, RANK // D, W), BF16),
             pltpu.VMEM((D // 2, RANK // D, W), BF16),
             pltpu.VMEM((D // 2, RANK // D, W), BF16),
@@ -565,6 +587,7 @@
             dma((NC, T // 4)), dma((NC, T // 4)),
             dma((NC,)), dma((NC,)),
             dma((NC, D)), dma((NC, D)),
+            dma((D // 2,)), dma((D // 2,)), dma((1,)), dma((1,)),
             dma((D // 2,)), dma((D // 2,)), dma((1,)), dma((1,)),
             dma((D // 2,)), dma((D // 2,)), dma((1,)), dma((1,)),
             dma((T,)), dma((T,)),

time: 153 us -> 152 us (level)
  no operation moved by 1% of the time
where the time goes in v4:
time: 152 us; the launch traced here: 151 us
  Pallas kernels  151 us (99%)
    pallas_call x1, Pallas kernels, local(): pl.pallas_call(functools.partial(kernel, dims), out_shape=(jax.ShapeDtype...  146 us
    pallas_call x1, Pallas kernels, local(): pl.pallas_call(functools.partial(deliver, n), out_shape=tuple((jax.ShapeD...  4.68 us

profile of v4, /device:TPU:1, one launch (start us, length us, event | category | flops | bytes accessed | tf_op | source)
XLA Modules:
  0.0 151.5 jit_solution(14872933926665144475)
XLA Ops:
  0.6 146.1 %shard_map.186 = (bf16[16,8,64,256]{3,2,1,0:T(8,128)(2,1)}, f32[256,256]{1,0:T(8,128)}, f32[32,2048]{1,0:T(8,128)}, f32[1,256]{1,0:T(1,128)}, f32[256,128]{1,0:T...) custom-call(bf16[16,8,64,256]{3,2,1,0:T(8,128)(2,1)} %bitcast.13, ...), custom_call_target="tpu_custom_call" | custom-call | tf_op jit(solution)/shard_map/pallas_call | solution.py:526
  146.8 4.7 %shard_map.187 = (bf16[16,8,64,256]{3,2,1,0:T(8,128)(2,1)}, f32[256,256]{1,0:T(8,128)}, f32[32,2048]{1,0:T(8,128)}, f32[1,256]{1,0:T(1,128)}, f32[256,128]{1,0:T...) custom-call(bf16[16,8,64,256]{3,2,1,0:T(8,128)(2,1)} %get-tuple-elem, ...), custom_call_target="tpu_custom_call" | custom-call | tf_op jit(solution)/shard_map/pallas_call | solution.py:604
